TPU v7x, 512 devices: a whole 4x4x16 slice. The times are simulated.
512 devices in a mesh: tm: 8 (over z_lo), height: 64 (over z_hi, y, x, core).
Axes of the slice: x: 4, y: 4, z: 16 (z_hi: 2, z_lo: 8; z = z_hi * 8 + z_lo), core: 2. Of those that a mesh axis runs over, the one named last changes fastest.
Arguments:
- features: bfloat16 [96, 32, 256, 128], P(None, 'tm', 'height'), may hold values from -6 to 6
- first_gain: float32 [96], replicated, may hold values from 0.1 to 1.9
- first_weight: bfloat16 [96, 2592], replicated, may hold values from -0.125 to 0.125
- first_bias: float32 [96], replicated, may hold values from -3 to 3
- second_gain: float32 [96], replicated, may hold values from 0.1 to 1.9
- second_weight: bfloat16 [96, 2592], replicated, may hold values from -0.125 to 0.125
- second_bias: float32 [96], replicated, may hold values from -3 to 3
Outputs:
- encoded: bfloat16 [96, 32, 256, 128], P(None, 'tm', 'height')
All inputs are finite; a program needn't handle non-finite values.
Results may differ from a plain program's by a relative error of at most 0.0036.
Values may be sent and summed in bfloat16 or wider, within the bound.
No kernel may reach another device: no remote copies, remote signals or barrier semaphores. Data moves between devices by JAX's collectives and lax.ppermute only.
A program may use at most 64 MiB of HBM per device.

v0:
```python
import jax
import jax.numpy as jnp
from jax import lax
from jax.sharding import PartitionSpec as P


def with_halo(block, sides, width):
    for axis, dim in sides:
        count = lax.axis_size(axis)
        forward = [(i, i + 1) for i in range(count - 1)]
        backward = [(target, source) for source, target in forward]
        low = lax.ppermute(
            lax.slice_in_dim(block, block.shape[dim] - width, None, axis=dim), axis, forward
        )
        high = lax.ppermute(lax.slice_in_dim(block, 0, width, axis=dim), axis, backward)
        block = jnp.concatenate([low, block, high], axis=dim)
    return block


def shifted(block, axis, distance):
    devices = range(lax.axis_size(axis))
    route = [(i - distance, i) for i in devices if i - distance in devices]
    return lax.ppermute(block, axis, route)


def activate(values, gain_vector):
    mean_square = jnp.mean(values * values, axis=0, keepdims=True)
    scaled = values * lax.rsqrt(mean_square + 1e-06) * gain_vector[:, None, None, None]
    return jax.nn.silu(scaled).astype(jnp.bfloat16)


def widen_rows(extended):
    return with_halo(extended, (("height", 2),), 1)


def valid_conv(padded, weight, bias_vector):
    channels = weight.shape[0]
    frames_out = padded.shape[1] - 2
    rows_out = padded.shape[2] - 2
    columns = padded.shape[3]
    widened = jnp.pad(padded, ((0, 0), (0, 0), (0, 0), (1, 1)))
    running = jnp.broadcast_to(
        bias_vector[:, None, None, None], (channels, frames_out, rows_out, columns)
    )
    for time_tap in range(3):
        window = widened[:, time_tap : time_tap + frames_out]
        stacked = jnp.concatenate(
            [window[..., column_tap : column_tap + columns] for column_tap in range(3)], axis=0
        )
        for row_tap in range(3):
            offset = (time_tap * 3 + row_tap) * 3 * channels
            tap_weight = weight[:, offset : offset + 3 * channels]
            running = running + jnp.einsum(
                "oi,ifrw->ofrw",
                tap_weight,
                stacked[:, :, row_tap : row_tap + rows_out],
                preferred_element_type=jnp.float32,
            )
    return running


def layer_conv(inputs, weight, bias_vector):
    earlier = shifted(inputs[:, -2:], "tm", 1)
    padded = widen_rows(jnp.concatenate([earlier, inputs], axis=1))
    return valid_conv(padded, weight, bias_vector)


def local(features, first_gain, first_weight, first_bias, second_gain, second_weight, second_bias):
    first_act = activate(features.astype(jnp.float32), first_gain)
    hidden = layer_conv(first_act, first_weight, first_bias)
    second_act = activate(hidden, second_gain)
    branch = layer_conv(second_act, second_weight, second_bias)
    return (features.astype(jnp.float32) + branch).astype(jnp.bfloat16)


def solution(mesh):
    return jax.shard_map(
        local,
        mesh=mesh,
        in_specs=(P(None, "tm", "height", None), P(), P(), P(), P(), P(), P()),
        out_specs=P(None, "tm", "height", None),
        check_vma=False,
    )
```

profile of v0, /device:TPU:63, one launch (start us, length us, event | category | flops | bytes accessed | tf_op | source)
XLA Modules:
  0.0 98.6 jit_solution(1658176004755989418)
XLA Ops:
  0.0 1.1 %fusion.21 = f32[4,4,128]{2,1,0:T(4,128)S(1)} fusion(bf16[96,4,4,128]{3,2,1,0:T(4,128)(2,1)} %param.7), kind=kLoop, calls=%fused_computation.61 | loop fusion | flops 587776 | bytes 401408 | tf_op jit(solution)/shard_map/reduce_sum | solution.py:27
  1.1 1.3 %fusion.28 = bf16[96,4,4,128]{3,0,2,1:T(8,128)(2,1)S(1)} fusion(f32[96]{0:T(128)} %param.8, f32[4,4,128]{2,1,0:T(4,128)S(1)} %add_rsqrt_fusion.1, bf16[96,4,4,128]{3,2,1,0:T(4,128)(2,1)} %param.7), kind=kLoop, calls=%fused_computation.68 | loop fusion | flops 1572864 | bytes 795008 | tf_op jit(solution)/shard_map/convert_element_type | solution.py:29
  2.5 3.5 %collective-permute-start = (bf16[96,2,4,128]{3,0,2,1:T(8,128)(2,1)S(1)}, bf16[96,2,4,128]{3,0,2,1:T(8,128)(2,1)S(1)}, u32[]{:S(2)}, u32[]{:S(2)}) collective-permute-start(bf16[96,2,4,128]{3,0,2,1:T(8,128)(2,1)S(1)} %slice.270), channel_id=1, source_target_pairs={{0,64},{64,128},{128,192},{192,256},{256,320},{320,384},{384,448},... | collective-permute-start | bytes 589832 | tf_op jit(solution)/shard_map/ppermute | solution.py:23
  6.0 4.1 %collective-permute-done = bf16[96,2,4,128]{3,0,2,1:T(8,128)(2,1)S(1)} collective-permute-done((bf16[96,2,4,128]{3,0,2,1:T(8,128)(2,1)S(1)}, bf16[96,2,4,128]{3,0,2,1:T(8,128)(2,1)S(1)}, u32[]{:S(2)}, u32[]{:S(2)}) %collective-permute-start) | collective-permute-done | bytes 196640 | tf_op jit(solution)/shard_map/ppermute | solution.py:23
  10.2 15.5 %collective-permute-start.1 = (bf16[96,6,1,128]{3,0,2,1:T(8,128)(2,1)S(1)}, bf16[96,6,1,128]{3,0,2,1:T(8,128)(2,1)S(1)}, u32[]{:S(2)}, u32[]{:S(2)}) collective-permute-start(bf16[96,6,1,128]{3,0,2,1:T(8,128)(2,1)S(1)} %get-tuple-element.25), channel_id=1, source_target_pairs={{0,1},{1,2},{2,3},{3,4},{4,5},{5,6},{6,7},{7,8},{8,9},{9,10},{10,1... | collective-permute-start | bytes 442376 | tf_op jit(solution)/shard_map/ppermute | solution.py:12
  25.7 1.9 %collective-permute-start.2 = (bf16[96,6,1,128]{3,0,2,1:T(8,128)(2,1)S(1)}, bf16[96,6,1,128]{3,0,2,1:T(8,128)(2,1)S(1)}, u32[]{:S(2)}, u32[]{:S(2)}) collective-permute-start(bf16[96,6,1,128]{3,0,2,1:T(8,128)(2,1)S(1)} %get-tuple-element.26), channel_id=1, source_target_pairs={{1,0},{2,1},{3,2},{4,3},{5,4},{6,5},{7,6},{8,7},{9,8},{10,9},{11,1... | collective-permute-start | bytes 442376 | tf_op jit(solution)/shard_map/ppermute | solution.py:15
  27.7 4.9 %collective-permute-done.1 = bf16[96,6,1,128]{3,0,2,1:T(8,128)(2,1)S(1)} collective-permute-done((bf16[96,6,1,128]{3,0,2,1:T(8,128)(2,1)S(1)}, bf16[96,6,1,128]{3,0,2,1:T(8,128)(2,1)S(1)}, u32[]{:S(2)}, u32[]{:S(2)}) %collective-permute-start.1) | collective-permute-done | bytes 147488 | tf_op jit(solution)/shard_map/ppermute | solution.py:12
  32.5 17.3 %collective-permute-done.2 = bf16[96,6,1,128]{3,0,2,1:T(8,128)(2,1)S(1)} collective-permute-done((bf16[96,6,1,128]{3,0,2,1:T(8,128)(2,1)S(1)}, bf16[96,6,1,128]{3,0,2,1:T(8,128)(2,1)S(1)}, u32[]{:S(2)}, u32[]{:S(2)}) %collective-permute-start.2) | collective-permute-done | bytes 147488 | tf_op jit(solution)/shard_map/ppermute | solution.py:15
  49.9 0.1 pad_maximum_fusion.6
  50.0 1.2 %pad_slice_fusion.7 = (bf16[96,4,6,128]{3,0,2,1:T(8,128)(2,1)S(1)}, bf16[96,4,6,128]{3,0,2,1:T(8,128)(2,1)S(1)}, bf16[96,4,6,128]{3,0,2,1:T(8,128)(2,1)S(1)}, bf...) fusion(bf16[96,6,6,128]{3,0,2,1:T(8,128)(2,1)S(1)} %pad_maximum, ...), kind=kLoop, calls=%fused_computation.7 | loop fusion | bytes 7962624 | tf_op jit(solution)/shard_map/slice | solution.py:48
  51.2 0.0 copy-start.1
  51.3 0.0 copy-start.3
  51.3 0.3 pad_maximum_fusion
  51.6 0.7 copy-done.1
  52.3 0.0 copy-done.3
  52.3 0.4 convolution_add_fusion.17
  52.7 0.5 convolution_add_fusion.16
  53.2 0.5 convolution_add_fusion.15
  53.7 0.5 convolution_add_fusion.14
  54.1 0.4 convolution_add_fusion.13
  54.6 0.5 convolution_add_fusion.12
  55.0 0.1 pad_maximum_fusion.2
  55.2 0.5 convolution_add_fusion.11
  55.6 0.5 convolution_add_fusion.10
  56.1 0.0 copy-start.4
  56.1 0.4 multiply_reduce_fusion
  56.6 0.2 copy-done.4
  56.8 0.3 fusion.32
  57.1 1.9 %collective-permute-start.3 = (bf16[96,2,4,128]{3,0,2,1:T(8,128)(2,1)S(1)}, bf16[96,2,4,128]{3,0,2,1:T(8,128)(2,1)S(1)}, u32[]{:S(2)}, u32[]{:S(2)}) collective-permute-start(bf16[96,2,4,128]{3,0,2,1:T(8,128)(2,1)S(1)} %slice.283), channel_id=1, source_target_pairs={{0,64},{64,128},{128,192},{192,256},{256,320},{320,384},{384,448},... | collective-permute-start | bytes 589832 | tf_op jit(solution)/shard_map/ppermute | solution.py:23
  59.0 4.5 %collective-permute-done.3 = bf16[96,2,4,128]{3,0,2,1:T(8,128)(2,1)S(1)} collective-permute-done((bf16[96,2,4,128]{3,0,2,1:T(8,128)(2,1)S(1)}, bf16[96,2,4,128]{3,0,2,1:T(8,128)(2,1)S(1)}, u32[]{:S(2)}, u32[]{:S(2)}) %collective-permute-start.3) | collective-permute-done | bytes 196640 | tf_op jit(solution)/shard_map/ppermute | solution.py:23
  63.6 2.9 %collective-permute-start.4 = (bf16[96,6,1,128]{3,0,2,1:T(8,128)(2,1)S(1)}, bf16[96,6,1,128]{3,0,2,1:T(8,128)(2,1)S(1)}, u32[]{:S(2)}, u32[]{:S(2)}) collective-permute-start(bf16[96,6,1,128]{3,0,2,1:T(8,128)(2,1)S(1)} %get-tuple-element.23), channel_id=1, source_target_pairs={{0,1},{1,2},{2,3},{3,4},{4,5},{5,6},{6,7},{7,8},{8,9},{9,10},{10,1... | collective-permute-start | bytes 442376 | tf_op jit(solution)/shard_map/ppermute | solution.py:12
  66.5 1.9 %collective-permute-start.5 = (bf16[96,6,1,128]{3,0,2,1:T(8,128)(2,1)S(1)}, bf16[96,6,1,128]{3,0,2,1:T(8,128)(2,1)S(1)}, u32[]{:S(2)}, u32[]{:S(2)}) collective-permute-start(bf16[96,6,1,128]{3,0,2,1:T(8,128)(2,1)S(1)} %get-tuple-element.24), channel_id=1, source_target_pairs={{1,0},{2,1},{3,2},{4,3},{5,4},{6,5},{7,6},{8,7},{9,8},{10,9},{11,1... | collective-permute-start | bytes 442376 | tf_op jit(solution)/shard_map/ppermute | solution.py:15
  68.4 4.6 %collective-permute-done.4 = bf16[96,6,1,128]{3,0,2,1:T(8,128)(2,1)S(1)} collective-permute-done((bf16[96,6,1,128]{3,0,2,1:T(8,128)(2,1)S(1)}, bf16[96,6,1,128]{3,0,2,1:T(8,128)(2,1)S(1)}, u32[]{:S(2)}, u32[]{:S(2)}) %collective-permute-start.4) | collective-permute-done | bytes 147488 | tf_op jit(solution)/shard_map/ppermute | solution.py:12
  73.1 17.3 %collective-permute-done.5 = bf16[96,6,1,128]{3,0,2,1:T(8,128)(2,1)S(1)} collective-permute-done((bf16[96,6,1,128]{3,0,2,1:T(8,128)(2,1)S(1)}, bf16[96,6,1,128]{3,0,2,1:T(8,128)(2,1)S(1)}, u32[]{:S(2)}, u32[]{:S(2)}) %collective-permute-start.5) | collective-permute-done | bytes 147488 | tf_op jit(solution)/shard_map/ppermute | solution.py:15
  90.4 0.1 pad_maximum_fusion.7
  90.5 1.2 %pad_slice_fusion.1 = (bf16[96,4,6,128]{3,0,2,1:T(8,128)(2,1)S(1)}, bf16[96,4,6,128]{3,0,2,1:T(8,128)(2,1)S(1)}, bf16[96,4,6,128]{3,0,2,1:T(8,128)(2,1)S(1)}, bf...) fusion(bf16[96,6,6,128]{3,0,2,1:T(8,128)(2,1)S(1)} %pad_maximum, ...), kind=kLoop, calls=%fused_computation.1 | loop fusion | bytes 7962624 | tf_op jit(solution)/shard_map/slice | solution.py:48
  91.8 0.0 copy-start.2
  91.8 0.0 copy-start.5
  91.8 0.1 pad_maximum_fusion.3
  91.9 0.9 copy-done.2
  92.8 0.0 copy-done.5
  92.8 0.4 convolution_add_fusion.8
  93.2 0.5 convolution_add_fusion.7
  93.7 0.5 convolution_add_fusion.6
  94.2 0.1 pad_maximum_fusion.4
  94.3 0.5 convolution_add_fusion.5
  94.8 0.4 convolution_add_fusion.4
  95.2 0.5 convolution_add_fusion.3
  95.7 0.1 pad_maximum_fusion.5
  95.8 0.5 convolution_add_fusion.2
  96.3 0.0 copy-start
  96.3 0.5 convolution_add_fusion.1
  96.8 0.5 copy-done
  97.3 0.4 fusion.2
  97.7 0.9 copy.9
  (6 shorter events, 0.1 us)
Async XLA Ops:
  2.5 7.7 %collective-permute-start = (bf16[96,2,4,128]{3,0,2,1:T(8,128)(2,1)S(1)}, bf16[96,2,4,128]{3,0,2,1:T(8,128)(2,1)S(1)}, u32[]{:S(2)}, u32[]{:S(2)}) collective-permute-start(bf16[96,2,4,128]{3,0,2,1:T(8,128)(2,1)S(1)} %slice.270), channel_id=1, source_target_pairs={{0,64},{64,128},{128,192},{192,256},{256,320},{320,384},{384,448},... | collective-permute-start | bytes 589832 | tf_op jit(solution)/shard_map/ppermute | solution.py:23
  10.2 22.4 %collective-permute-start.1 = (bf16[96,6,1,128]{3,0,2,1:T(8,128)(2,1)S(1)}, bf16[96,6,1,128]{3,0,2,1:T(8,128)(2,1)S(1)}, u32[]{:S(2)}, u32[]{:S(2)}) collective-permute-start(bf16[96,6,1,128]{3,0,2,1:T(8,128)(2,1)S(1)} %get-tuple-element.25), channel_id=1, source_target_pairs={{0,1},{1,2},{2,3},{3,4},{4,5},{5,6},{6,7},{7,8},{8,9},{9,10},{10,1... | collective-permute-start | bytes 442376 | tf_op jit(solution)/shard_map/ppermute | solution.py:12
  25.7 24.1 %collective-permute-start.2 = (bf16[96,6,1,128]{3,0,2,1:T(8,128)(2,1)S(1)}, bf16[96,6,1,128]{3,0,2,1:T(8,128)(2,1)S(1)}, u32[]{:S(2)}, u32[]{:S(2)}) collective-permute-start(bf16[96,6,1,128]{3,0,2,1:T(8,128)(2,1)S(1)} %get-tuple-element.26), channel_id=1, source_target_pairs={{1,0},{2,1},{3,2},{4,3},{5,4},{6,5},{7,6},{8,7},{9,8},{10,9},{11,1... | collective-permute-start | bytes 442376 | tf_op jit(solution)/shard_map/ppermute | solution.py:15
  51.2 1.0 %copy-start.1 = (bf16[96,2592]{1,0:T(8,128)(2,1)S(1)}, bf16[96,2592]{1,0:T(8,128)(2,1)}, u32[]{:S(2)}) copy-start(bf16[96,2592]{1,0:T(8,128)(2,1)} %param.9) | copy-start | bytes 1492996
  51.3 1.0 %copy-start.3 = (f32[96]{0:T(128)S(1)}, f32[96]{0:T(128)}, u32[]{:S(2)}) copy-start(f32[96]{0:T(128)} %param.10) | copy-start | bytes 1156
  56.1 0.7 copy-start.4
  57.1 6.4 %collective-permute-start.3 = (bf16[96,2,4,128]{3,0,2,1:T(8,128)(2,1)S(1)}, bf16[96,2,4,128]{3,0,2,1:T(8,128)(2,1)S(1)}, u32[]{:S(2)}, u32[]{:S(2)}) collective-permute-start(bf16[96,2,4,128]{3,0,2,1:T(8,128)(2,1)S(1)} %slice.283), channel_id=1, source_target_pairs={{0,64},{64,128},{128,192},{192,256},{256,320},{320,384},{384,448},... | collective-permute-start | bytes 589832 | tf_op jit(solution)/shard_map/ppermute | solution.py:23
  63.6 9.5 %collective-permute-start.4 = (bf16[96,6,1,128]{3,0,2,1:T(8,128)(2,1)S(1)}, bf16[96,6,1,128]{3,0,2,1:T(8,128)(2,1)S(1)}, u32[]{:S(2)}, u32[]{:S(2)}) collective-permute-start(bf16[96,6,1,128]{3,0,2,1:T(8,128)(2,1)S(1)} %get-tuple-element.23), channel_id=1, source_target_pairs={{0,1},{1,2},{2,3},{3,4},{4,5},{5,6},{6,7},{7,8},{8,9},{9,10},{10,1... | collective-permute-start | bytes 442376 | tf_op jit(solution)/shard_map/ppermute | solution.py:12
  66.5 23.9 %collective-permute-start.5 = (bf16[96,6,1,128]{3,0,2,1:T(8,128)(2,1)S(1)}, bf16[96,6,1,128]{3,0,2,1:T(8,128)(2,1)S(1)}, u32[]{:S(2)}, u32[]{:S(2)}) collective-permute-start(bf16[96,6,1,128]{3,0,2,1:T(8,128)(2,1)S(1)} %get-tuple-element.24), channel_id=1, source_target_pairs={{1,0},{2,1},{3,2},{4,3},{5,4},{6,5},{7,6},{8,7},{9,8},{10,9},{11,1... | collective-permute-start | bytes 442376 | tf_op jit(solution)/shard_map/ppermute | solution.py:15
  91.8 1.0 %copy-start.2 = (bf16[96,2592]{1,0:T(8,128)(2,1)S(1)}, bf16[96,2592]{1,0:T(8,128)(2,1)}, u32[]{:S(2)}) copy-start(bf16[96,2592]{1,0:T(8,128)(2,1)} %param.12) | copy-start | bytes 1492996
  91.8 1.0 %copy-start.5 = (f32[96]{0:T(128)S(1)}, f32[96]{0:T(128)}, u32[]{:S(2)}) copy-start(f32[96]{0:T(128)} %param.13) | copy-start | bytes 1156
  96.3 1.0 %copy-start = (bf16[96,4,4,128]{3,2,1,0:T(4,128)(2,1)S(1)}, bf16[96,4,4,128]{3,2,1,0:T(4,128)(2,1)}, u32[]{:S(2)}) copy-start(bf16[96,4,4,128]{3,2,1,0:T(4,128)(2,1)} %param.7) | copy-start | bytes 1179652
where the time goes:
time: 99 us; the launch traced here: 98.6 us
  waiting for transfers between devices  52.8 us (53%)
  starting transfers between devices  27.8 us (28%)
  matrix products  8.19 us (8%)
  local copies, waits for them, and re-layouts  5.75 us (6%)
  other arithmetic  3.87 us (4%)
    ppermute x2, waiting for transfers between devices, with_halo(): lax.ppermute(lax.slice_in_dim(block, 0, width, axis=dim), axis, backward)  34.7 us
    ppermute x2, starting transfers between devices, with_halo(): lax.ppermute(lax.slice_in_dim(block, block.shape[dim] - width, None, axis...  18.5 us
    ppermute x2, waiting for transfers between devices, with_halo(): lax.ppermute(lax.slice_in_dim(block, block.shape[dim] - width, None, axis...  9.52 us
    ppermute x2, waiting for transfers between devices, shifted(): return lax.ppermute(block, axis, route)  8.6 us
    dot_general x18, matrix products, valid_conv(): jnp.einsum('oi,ifrw->ofrw', tap_weight, stacked[:, :, row_tap:row_tap + r...  8.19 us
    ppermute x2, starting transfers between devices, shifted(): return lax.ppermute(block, axis, route)  5.47 us
    ppermute x2, starting transfers between devices, with_halo(): lax.ppermute(lax.slice_in_dim(block, 0, width, axis=dim), axis, backward)  3.84 us
    slice x2, local copies, waits for them, and re-layouts, valid_conv(): window[..., column_tap:column_tap + columns]  2.47 us
  transfers between devices with their start and end apart: 6, of which 6 were waited for; matrix products, arithmetic and copies ran while one was open for 0% of the time, Pallas kernels for 0%

commit v1 on v0

v1 whole, which is shorter than its diff:
```python
import functools

import jax
import jax.numpy as jnp
from jax import lax
from jax.experimental import pallas as pl
from jax.experimental.pallas import tpu as pltpu
from jax.sharding import PartitionSpec as P

C = 96
W = 128
TAPS = 9 * C
BF16 = jnp.bfloat16
F32 = jnp.float32
VMEM = pl.BlockSpec(memory_space=pltpu.VMEM)
PARAMS = pltpu.CompilerParams(vmem_limit_bytes=24 * 1024 * 1024)


def column(row):
    here = lax.broadcasted_iota(jnp.int32, (C, C), 0) == lax.broadcasted_iota(jnp.int32, (C, C), 1)
    return jnp.sum(jnp.where(here, row, 0.0), axis=1, keepdims=True)


def activation(values, gain):
    mean_square = jnp.sum(values * values, axis=0, keepdims=True) * (1.0 / C)
    scaled = values * lax.rsqrt(mean_square + 1e-06) * gain
    return scaled * (1.0 / (1.0 + jnp.exp(-scaled)))


def orientation():
    odd = lax.rem(lax.axis_index("height"), 2)
    return odd, 1 - 2 * odd


def natural(row, odd):
    return row + odd * (3 - 2 * row)


def first_act_kernel(features, gain_row, act, wide):
    odd, _ = orientation()
    gain = jnp.broadcast_to(column(gain_row[...]), (C, W))
    wide[...] = features[...].astype(F32)
    for frame in range(4):
        for row in range(4):
            values = wide[pl.ds(frame * 4 + row, C, stride=16), :]
            act[frame, natural(row, odd)] = activation(values, gain).astype(BF16)


def weight_kernel(first, second, first_bias, second_gain, second_bias, first_out, second_out, columns):
    for step, row in enumerate((first_bias, second_gain, second_bias)):
        columns[step] = jnp.broadcast_to(column(row[...]), (C, W))
    for source, target in ((first, first_out), (second, second_out)):
        for time_row in range(9):
            for tap in range(3):
                offset = (time_row * 3 + tap) * C
                target[tap * C : (tap + 1) * C, time_row * C : (time_row + 1) * C] = source[
                    :, offset : offset + C
                ]


def conv_pair(acts, weight, bias, frame, row, sign):
    columns = []
    for centre in (row, row + 1):
        blocks = [acts[frame + p, centre + sign * (q - 1)] for p in range(3) for q in range(3)]
        columns.append(jnp.concatenate(blocks, axis=0))
    stacked = jnp.concatenate(columns, axis=1)
    sums = jnp.dot(weight[...], stacked, preferred_element_type=F32)
    lane = lax.broadcasted_iota(jnp.int32, (C, W), 1)
    results = []
    for half in range(2):
        part = sums[:, half * W : (half + 1) * W]
        left = jnp.where(lane == 0, 0.0, pltpu.roll(part[:C], 1, 1))
        right = jnp.where(lane == W - 1, 0.0, pltpu.roll(part[2 * C :], W - 1, 1))
        results.append(part[C : 2 * C] + left + right + bias)
    return results


def near_kernel(
    own, earlier, even, first_weight, second_weight, columns,
    hidden_out, branch_out, acts, hidden,
):
    _, sign = orientation()
    started = lax.axis_index("tm") > 0
    for frame in range(4):
        acts[frame, 0:4] = earlier[frame]
        acts[frame + 4, 0:4] = own[frame]
    for frame in range(8):
        acts[frame, 4] = even[frame, 1]
        acts[frame, 5] = even[frame, 0]
    bias, gain, last_bias = columns[0], columns[1], columns[2]

    @pl.loop(0, 6)
    def _(frame):
        inside = jnp.logical_or(started, frame >= 2)
        for row in (1, 3):
            pair = conv_pair(acts, first_weight, bias, frame, row, sign)
            for step, values in enumerate(pair):
                result = jnp.where(inside, activation(values, gain), 0.0).astype(BF16)
                hidden[frame, row - 1 + step] = result
                if row == 1:
                    hidden_out[frame, step] = result

    @pl.loop(0, 4)
    def _(frame):
        pair = conv_pair(hidden, second_weight, last_bias, frame, 1, sign)
        for step, values in enumerate(pair):
            branch_out[frame, step] = values


def far_kernel(
    features, own, earlier, far, far_earlier, near_hidden, near_branch,
    first_weight, second_weight, columns,
    encoded, acts, hidden, total,
):
    odd, sign = orientation()
    started = lax.axis_index("tm") > 0
    height = lax.axis_index("height")
    bordered = jnp.logical_or(height == 0, height == lax.axis_size("height") - 1)
    for frame in range(4):
        for step in range(2):
            acts[frame, 1 - step] = far_earlier[frame, step]
            acts[frame + 4, 1 - step] = far[frame, step]
            acts[frame, 2 + step] = earlier[frame, step]
            acts[frame + 4, 2 + step] = own[frame, step]
    for frame in range(6):
        hidden[frame, 2:4] = near_hidden[frame]
    bias, gain, last_bias = columns[0], columns[1], columns[2]

    @pl.loop(0, 6)
    def _(frame):
        inside = jnp.logical_or(started, frame >= 2)
        pair = conv_pair(acts, first_weight, bias, frame, 1, sign)
        for step, values in enumerate(pair):
            keep = jnp.logical_and(inside, jnp.logical_not(bordered)) if step == 0 else inside
            hidden[frame, step] = jnp.where(keep, activation(values, gain), 0.0).astype(BF16)

    @pl.loop(0, 4)
    def _(frame):
        pair = conv_pair(hidden, second_weight, last_bias, frame, 1, sign)
        for step, values in enumerate(pair):
            total[pl.ds(frame * 4 + natural(step, odd), C, stride=16), :] = values
            total[pl.ds(frame * 4 + natural(step + 2, odd), C, stride=16), :] = near_branch[frame, step]

    encoded[...] = (features[...].astype(F32) + total[...]).astype(BF16)


def shape(*dims, dtype=BF16):
    return jax.ShapeDtypeStruct(dims, dtype)


def call(kernel, out_shape, scratch, inputs, **kwargs):
    many = isinstance(out_shape, (list, tuple))
    return pl.pallas_call(
        kernel,
        out_shape=out_shape,
        in_specs=[VMEM] * len(inputs),
        out_specs=[VMEM] * len(out_shape) if many else VMEM,
        scratch_shapes=scratch,
        compiler_params=PARAMS,
        **kwargs,
    )(*inputs)


def held(array, flops):
    return pl.pallas_call(
        lambda source, target: None,
        out_shape=jax.ShapeDtypeStruct(array.shape, array.dtype),
        in_specs=[pl.BlockSpec(memory_space=pl.ANY)],
        out_specs=pl.BlockSpec(memory_space=pl.ANY),
        input_output_aliases={0: 0},
        compiler_params=pltpu.CompilerParams(vmem_limit_bytes=1 << 20),
        cost_estimate=pl.CostEstimate(flops=flops, bytes_accessed=0, transcendentals=0),
    )(array)


def swap_pairs(first, count):
    edges = [(i, i + 1) for i in range(first, count - 1, 2)]
    return edges + [(b, a) for a, b in edges]


def local(features, first_gain, first_weight, first_bias, second_gain, second_weight, second_bias):
    height, times = lax.axis_size("height"), lax.axis_size("tm")
    later = [(i, i + 1) for i in range(times - 1)]
    flat = features.reshape(C * 16, W)
    rows = [v.reshape(1, C) for v in (first_bias, second_gain, second_bias)]

    act = call(
        first_act_kernel, shape(4, 4, C, W), [pltpu.VMEM((C * 16, W), F32)],
        (flat, first_gain.reshape(1, C)),
    )
    far = lax.ppermute(act[:, 0:2], "height", swap_pairs(1, height))
    prepared = call(
        weight_kernel,
        [shape(3 * C, TAPS), shape(3 * C, TAPS), shape(3, C, W, dtype=F32)], [],
        (first_weight, second_weight, *rows),
        cost_estimate=pl.CostEstimate(flops=1 << 35, bytes_accessed=1 << 21, transcendentals=0),
    )
    earlier = lax.ppermute(act, "tm", later)
    both = jnp.concatenate([earlier[:, 2:4], act[:, 2:4]], axis=0)
    both, prepared = lax.optimization_barrier((both, prepared))
    even = lax.ppermute(both, "height", swap_pairs(0, height))
    far = held(far, 1 << 33)
    far, even = lax.optimization_barrier((far, even))
    far_earlier = lax.ppermute(far, "tm", later)
    near_hidden, near_branch = call(
        near_kernel, [shape(6, 2, C, W), shape(4, 2, C, W, dtype=F32)],
        [pltpu.VMEM((8, 6, C, W), BF16), pltpu.VMEM((6, 4, C, W), BF16)],
        (act, earlier, even, *prepared),
        cost_estimate=pl.CostEstimate(flops=32 * W * C * TAPS * 6, bytes_accessed=1 << 21, transcendentals=0),
    )
    encoded = call(
        far_kernel, shape(C * 16, W),
        [pltpu.VMEM((8, 4, C, W), BF16), pltpu.VMEM((6, 4, C, W), BF16), pltpu.VMEM((C * 16, W), F32)],
        (flat, act, earlier, far, far_earlier, near_hidden, near_branch, *prepared),
        cost_estimate=pl.CostEstimate(flops=20 * W * C * TAPS * 6, bytes_accessed=1 << 21, transcendentals=0),
    )
    return encoded.reshape(features.shape)


def solution(mesh):
    return jax.shard_map(
        local,
        mesh=mesh,
        in_specs=(P(None, "tm", "height", None), P(), P(), P(), P(), P(), P()),
        out_specs=P(None, "tm", "height", None),
        check_vma=False,
    )
```

time: 99 us -> 47.5 us (0.48)
  the two profiles are of different devices: /device:TPU:63 before, /device:TPU:191 now
where the time goes in v1:
time: 47.5 us; the launch traced here: 47.3 us
  starting transfers between devices  22.9 us (48%)
  Pallas kernels  12.3 us (26%)
  waiting for transfers between devices  9.5 us (20%)
  local copies, waits for them, and re-layouts  2.35 us (5%)
    pallas_call x4, Pallas kernels, call(): pl.pallas_call(kernel, out_shape=out_shape, in_specs=[VMEM] * len(inputs)...  12.3 us
    ppermute x1, waiting for transfers between devices, local(): far = lax.ppermute(act[:, 0:2], 'height', swap_pairs(1, height))  9.49 us
    ppermute x1, starting transfers between devices, local(): far = lax.ppermute(act[:, 0:2], 'height', swap_pairs(1, height))  9.25 us
    ppermute x1, starting transfers between devices, local(): far_earlier = lax.ppermute(far, 'tm', later)  8.09 us
    ppermute x1, starting transfers between devices, local(): earlier = lax.ppermute(act, 'tm', later)  3.68 us
    unnamed x16, local copies, waits for them, and re-layouts  2.31 us
    ppermute x1, starting transfers between devices, local(): even = lax.ppermute(both, 'height', swap_pairs(0, height))  1.92 us
  transfers between devices with their start and end apart: 4, of which 1 were waited for; matrix products, arithmetic and copies ran while one was open for 0% of the time, Pallas kernels for 13%

profile of v1, /device:TPU:191, one launch (start us, length us, event | category | flops | bytes accessed | tf_op | source)
XLA Modules:
  0.0 47.3 jit_solution(5197696452554399097)
XLA Ops:
  0.0 0.0 copy-start.2
  0.0 0.7 %copy-done.2 = f32[96]{0:T(128)S(1)} copy-done((f32[96]{0:T(128)S(1)}, f32[96]{0:T(128)}, u32[]{:S(2)}) %copy-start.2) | copy-done | bytes 408
  0.7 0.0 copy-start
  0.7 1.0 %copy-done = bf16[96,4,4,128]{3,2,1,0:T(4,128)(2,1)S(1)} copy-done((bf16[96,4,4,128]{3,2,1,0:T(4,128)(2,1)S(1)}, bf16[96,4,4,128]{3,2,1,0:T(4,128)(2,1)}, u32[]{:S(2)}) %copy-start) | copy-done | bytes 393240
  1.7 0.0 copy-start.4
  1.7 0.5 %shard_map.73.own = bf16[4,4,96,128]{3,2,1,0:T(8,128)(2,1)S(1)} custom-call(bf16[1536,128]{1,0:T(8,128)(2,1)S(1)} %bitcast.6, f32[1,96]{1,0:T(1,128)S(1)} %bitcast.8), custom_call_target="tpu_custom_call" | custom-call | tf_op jit(solution)/shard_map/pallas_call | solution.py:153
  2.2 0.0 copy-start.3
  2.2 3.7 %collective-permute-start = (bf16[4,4,96,128]{3,2,1,0:T(8,128)(2,1)S(1)}, bf16[4,4,96,128]{3,2,1,0:T(8,128)(2,1)S(1)}, u32[]{:S(2)}, u32[]{:S(2)}) collective-permute-start(bf16[4,4,96,128]{3,2,1,0:T(8,128)(2,1)S(1)} %shard_map.73.own), channel_id=1, source_target_pairs={{0,64},{64,128},{128,192},{192,256},{256,320},{320,384},{384,448},... | collective-permute-start | bytes 1179656 | tf_op jit(solution)/shard_map/ppermute | solution.py:198
  5.9 9.3 %collective-permute-start.1 = (bf16[4,2,96,128]{3,2,1,0:T(8,128)(2,1)S(1)}, bf16[4,2,96,128]{3,2,1,0:T(8,128)(2,1)S(1)}, u32[]{:S(2)}, u32[]{:S(2)}) collective-permute-start(bf16[4,2,96,128]{3,2,1,0:T(8,128)(2,1)S(1)} %get-tuple-element.28), channel_id=1, source_target_pairs={{1,2},{3,4},{5,6},{7,8},{9,10},{11,12},{13,14},{15,16},{17,18},{19... | collective-permute-start | bytes 589832 | tf_op jit(solution)/shard_map/ppermute | solution.py:191
  15.2 0.0 copy-start.5
  15.2 0.0 copy-start.6
  15.2 0.0 copy-start.7
  15.2 0.0 copy-done.4
  15.2 0.0 copy-done.3
  15.2 0.6 %copy-done.5 = f32[96]{0:T(128)S(1)} copy-done((f32[96]{0:T(128)S(1)}, f32[96]{0:T(128)}, u32[]{:S(2)}) %copy-start.5) | copy-done | bytes 408
  15.8 0.0 copy-done.6
  15.9 0.0 copy-done.7
  15.9 0.6 %shard_map.75 = (bf16[288,864]{1,0:T(8,128)(2,1)S(1)}, bf16[288,864]{1,0:T(8,128)(2,1)S(1)}, f32[3,96,128]{2,1,0:T(8,128)S(1)}) custom-call(bf16[96,2592]{1,0:T(8,128)(2,1)S(1)} %copy-done.3, bf16[96,2592]{1,0:T(8,128)(2,1)S(1)} %copy-done.4, f32[1,96]{1,0:T(1,128)S(1)} %bitcast.9, f32[1,96]{1,0:T(1,128)S(1)} %bitcast.10, f32[1,96]{1,0:T(1,128)S(1)} %bitcast.11), custom_call_target="tpu_custom_call" | custom-call | flops 34359738368 | bytes 2097152 | tf_op jit(solution)/shard_map/pallas_call | solution.py:153
  16.5 0.0 collective-permute-done.earlier
  16.5 1.9 %collective-permute-start.2 = (bf16[8,2,96,128]{3,2,1,0:T(8,128)(2,1)S(1)}, bf16[8,2,96,128]{3,2,1,0:T(8,128)(2,1)S(1)}, u32[]{:S(2)}, u32[]{:S(2)}) collective-permute-start(bf16[8,2,96,128]{3,2,1,0:T(8,128)(2,1)S(1)} %pad_maximum_fusion), channel_id=1, source_target_pairs={{0,1},{2,3},{4,5},{6,7},{8,9},{10,11},{12,13},{14,15},{16,17},{18,... | collective-permute-start | bytes 1179656 | tf_op jit(solution)/shard_map/ppermute | solution.py:201
  18.5 9.5 %collective-permute-done.1.source = bf16[4,2,96,128]{3,2,1,0:T(8,128)(2,1)S(1)} collective-permute-done((bf16[4,2,96,128]{3,2,1,0:T(8,128)(2,1)S(1)}, bf16[4,2,96,128]{3,2,1,0:T(8,128)(2,1)S(1)}, u32[]{:S(2)}, u32[]{:S(2)}) %collective-permute-start.1) | collective-permute-done | bytes 196640 | tf_op jit(solution)/shard_map/ppermute | solution.py:191
  28.0 0.0 copy-start.1
  28.0 0.0 collective-permute-done.2.even
  28.0 8.1 %collective-permute-start.3 = (bf16[4,2,96,128]{3,2,1,0:T(8,128)(2,1)S(1)}, bf16[4,2,96,128]{3,2,1,0:T(8,128)(2,1)S(1)}, u32[]{:S(2)}, u32[]{:S(2)}) collective-permute-start(bf16[4,2,96,128]{3,2,1,0:T(8,128)(2,1)S(1)} %shard_map.74.far), channel_id=1, source_target_pairs={{0,64},{64,128},{128,192},{192,256},{256,320},{320,384},{384,448},... | collective-permute-start | bytes 589832 | tf_op jit(solution)/shard_map/ppermute | solution.py:204
  36.1 5.6 %shard_map.76 = (bf16[6,2,96,128]{3,2,1,0:T(8,128)(2,1)S(1)}, f32[4,2,96,128]{3,2,1,0:T(8,128)S(1)}) custom-call(bf16[4,4,96,128]{3,2,1,0:T(8,128)(2,1)S(1)} %shard_map.73.own, bf16[4,4,96,128]{3,2,1,0:T(8,128)(2,1)S(1)} %collective-permute-done.earlier, bf16[8,2,96,128]{3,2,1,0:T(8,128)(2,1)S(1)} %collective-permute-done.2.even, ...), custom_call_target="tpu_custom_call" | custom-call | flops 2038431744 | bytes 2097152 | tf_op jit(solution)/shard_map/pallas_call | solution.py:153
  41.7 0.0 collective-permute-done.3.far_earlier
  41.7 0.0 copy-done.1
  41.7 5.6 %shard_map.77 = bf16[1536,128]{1,0:T(8,128)(2,1)} custom-call(bf16[1536,128]{1,0:T(8,128)(2,1)S(1)} %bitcast.7, bf16[4,4,96,128]{3,2,1,0:T(8,128)(2,1)S(1)} %shard_map.73.own, bf16[4,4,96,128]{3,2,1,0:T(8,128)(2,1)S(1)} %collective-permute-done.earlier, bf16[4,2,96,128]{3,2,1,0:T(8,128)(2,1)S(1)} %shard_map.74.far, ...), custom_call_target="tpu_custom_call" | custom-call | flops 1274019840 | bytes 2097152 | tf_op jit(solution)/shard_map/pallas_call | solution.py:153
  (4 shorter events, 0.1 us)
Async XLA Ops:
  0.0 0.7 %copy-start.2 = (f32[96]{0:T(128)S(1)}, f32[96]{0:T(128)}, u32[]{:S(2)}) copy-start(f32[96]{0:T(128)} %param.8) | copy-start | bytes 1156
  0.7 1.0 %copy-start = (bf16[96,4,4,128]{3,2,1,0:T(4,128)(2,1)S(1)}, bf16[96,4,4,128]{3,2,1,0:T(4,128)(2,1)}, u32[]{:S(2)}) copy-start(bf16[96,4,4,128]{3,2,1,0:T(4,128)(2,1)} %param.7) | copy-start | bytes 1179652
  1.7 13.6 %copy-start.4 = (bf16[96,2592]{1,0:T(8,128)(2,1)S(1)}, bf16[96,2592]{1,0:T(8,128)(2,1)}, u32[]{:S(2)}) copy-start(bf16[96,2592]{1,0:T(8,128)(2,1)} %second.1) | copy-start | bytes 1492996
  2.2 13.0 %copy-start.3 = (bf16[96,2592]{1,0:T(8,128)(2,1)S(1)}, bf16[96,2592]{1,0:T(8,128)(2,1)}, u32[]{:S(2)}) copy-start(bf16[96,2592]{1,0:T(8,128)(2,1)} %first.1) | copy-start | bytes 1492996
  2.2 14.3 %collective-permute-start = (bf16[4,4,96,128]{3,2,1,0:T(8,128)(2,1)S(1)}, bf16[4,4,96,128]{3,2,1,0:T(8,128)(2,1)S(1)}, u32[]{:S(2)}, u32[]{:S(2)}) collective-permute-start(bf16[4,4,96,128]{3,2,1,0:T(8,128)(2,1)S(1)} %shard_map.73.own), channel_id=1, source_target_pairs={{0,64},{64,128},{128,192},{192,256},{256,320},{320,384},{384,448},... | collective-permute-start | bytes 1179656 | tf_op jit(solution)/shard_map/ppermute | solution.py:198
  5.9 22.0 %collective-permute-start.1 = (bf16[4,2,96,128]{3,2,1,0:T(8,128)(2,1)S(1)}, bf16[4,2,96,128]{3,2,1,0:T(8,128)(2,1)S(1)}, u32[]{:S(2)}, u32[]{:S(2)}) collective-permute-start(bf16[4,2,96,128]{3,2,1,0:T(8,128)(2,1)S(1)} %get-tuple-element.28), channel_id=1, source_target_pairs={{1,2},{3,4},{5,6},{7,8},{9,10},{11,12},{13,14},{15,16},{17,18},{19... | collective-permute-start | bytes 589832 | tf_op jit(solution)/shard_map/ppermute | solution.py:191
  15.2 0.7 %copy-start.5 = (f32[96]{0:T(128)S(1)}, f32[96]{0:T(128)}, u32[]{:S(2)}) copy-start(f32[96]{0:T(128)} %param.10) | copy-start | bytes 1156
  15.2 0.7 %copy-start.6 = (f32[96]{0:T(128)S(1)}, f32[96]{0:T(128)}, u32[]{:S(2)}) copy-start(f32[96]{0:T(128)} %param.11) | copy-start | bytes 1156
  15.2 0.7 %copy-start.7 = (f32[96]{0:T(128)S(1)}, f32[96]{0:T(128)}, u32[]{:S(2)}) copy-start(f32[96]{0:T(128)} %param.13) | copy-start | bytes 1156
  16.5 11.4 %collective-permute-start.2 = (bf16[8,2,96,128]{3,2,1,0:T(8,128)(2,1)S(1)}, bf16[8,2,96,128]{3,2,1,0:T(8,128)(2,1)S(1)}, u32[]{:S(2)}, u32[]{:S(2)}) collective-permute-start(bf16[8,2,96,128]{3,2,1,0:T(8,128)(2,1)S(1)} %pad_maximum_fusion), channel_id=1, source_target_pairs={{0,1},{2,3},{4,5},{6,7},{8,9},{10,11},{12,13},{14,15},{16,17},{18,... | collective-permute-start | bytes 1179656 | tf_op jit(solution)/shard_map/ppermute | solution.py:201
  28.0 13.8 %copy-start.1 = (bf16[96,4,4,128]{3,2,1,0:T(4,128)(2,1)S(1)}, bf16[96,4,4,128]{3,2,1,0:T(4,128)(2,1)}, u32[]{:S(2)}) copy-start(bf16[96,4,4,128]{3,2,1,0:T(4,128)(2,1)} %param.7) | copy-start | bytes 1179652
  28.0 13.7 %collective-permute-start.3 = (bf16[4,2,96,128]{3,2,1,0:T(8,128)(2,1)S(1)}, bf16[4,2,96,128]{3,2,1,0:T(8,128)(2,1)S(1)}, u32[]{:S(2)}, u32[]{:S(2)}) collective-permute-start(bf16[4,2,96,128]{3,2,1,0:T(8,128)(2,1)S(1)} %shard_map.74.far), channel_id=1, source_target_pairs={{0,64},{64,128},{128,192},{192,256},{256,320},{320,384},{384,448},... | collective-permute-start | bytes 589832 | tf_op jit(solution)/shard_map/ppermute | solution.py:204

commit v2 on v1

v2 whole, which is shorter than its diff:
```python
import functools

import jax
import jax.numpy as jnp
from jax import lax
from jax.experimental import pallas as pl
from jax.experimental.pallas import tpu as pltpu
from jax.sharding import PartitionSpec as P

C = 96
W = 128
TAPS = 9 * C
BF16 = jnp.bfloat16
F32 = jnp.float32
VMEM = pl.BlockSpec(memory_space=pltpu.VMEM)
PARAMS = pltpu.CompilerParams(vmem_limit_bytes=24 * 1024 * 1024)


def column(row):
    here = lax.broadcasted_iota(jnp.int32, (C, C), 0) == lax.broadcasted_iota(jnp.int32, (C, C), 1)
    return jnp.sum(jnp.where(here, row, 0.0), axis=1, keepdims=True)


def activation(values, gain):
    mean_square = jnp.sum(values * values, axis=0, keepdims=True) * (1.0 / C)
    scaled = values * lax.rsqrt(mean_square + 1e-06) * gain
    return scaled * (1.0 / (1.0 + jnp.exp(-scaled)))


def natural(row):
    return row + lax.rem(lax.axis_index("height"), 2) * (3 - 2 * row)


def first_act_kernel(features_in, gain_in, edge, act, sent, features, gain_row, wide, arrived):
    copies = [
        pltpu.make_async_copy(features_in, features, arrived.at[0]),
        pltpu.make_async_copy(gain_in, gain_row, arrived.at[1]),
    ]
    for copy in copies:
        copy.start()
    for copy in copies:
        copy.wait()
    gain = jnp.broadcast_to(column(gain_row[...]), (C, W))
    wide[...] = features[...].astype(F32)
    for frame in range(4):
        for row in range(4):
            values = wide[pl.ds(frame * 4 + row, C, stride=16), :]
            result = activation(values, gain).astype(BF16)
            act[frame, natural(row)] = result
    edge[...] = act[:, 0:2]
    sent[...] = act[...]


def weight_kernel(first, second, first_bias, second_gain, second_bias, *targets):
    columns = targets[-1]
    for step, row in enumerate((first_bias, second_gain, second_bias)):
        columns[step] = jnp.broadcast_to(column(row[...]), (C, W))
    reversed_rows = lax.rem(lax.axis_index("height"), 2) == 1
    for source, (whole, late, last) in ((first, targets[0:3]), (second, targets[3:6])):
        for row_tap in range(3):
            for time_tap in range(3):
                place = (row_tap * 3 + time_tap) * C
                for tap in range(3):
                    offset = ((time_tap * 3 + row_tap) * 3 + tap) * C
                    mirrored = ((time_tap * 3 + 2 - row_tap) * 3 + tap) * C
                    block = jnp.where(
                        reversed_rows, source[:, mirrored : mirrored + C], source[:, offset : offset + C]
                    )
                    lines = slice(tap * C, (tap + 1) * C)
                    whole[lines, place : place + C] = block
                    if row_tap >= 1:
                        late[lines, place - 3 * C : place - 2 * C] = block
                    if row_tap == 2:
                        last[lines, place - 6 * C : place - 5 * C] = block


def products(weight, left, right):
    stacked = jnp.concatenate([jnp.concatenate(left, axis=0), jnp.concatenate(right, axis=0)], axis=1)
    sums = jnp.dot(weight, stacked, preferred_element_type=F32)
    lane = lax.broadcasted_iota(jnp.int32, (C, W), 1)
    results = []
    for half in range(2):
        part = sums[:, half * W : (half + 1) * W]
        before = jnp.where(lane == 0, 0.0, pltpu.roll(part[:C], 1, 1))
        after = jnp.where(lane == W - 1, 0.0, pltpu.roll(part[2 * C :], W - 1, 1))
        results.append(part[C : 2 * C] + before + after)
    return results


def window(cell, frame, rows):
    return [cell(frame + step, row) for row in rows for step in range(3)]


def borders():
    height = lax.axis_index("height")
    outer = jnp.logical_or(height == 0, height == lax.axis_size("height") - 1)
    return lax.axis_index("tm") > 0, jnp.logical_not(outer)


def near_kernel(
    own, earlier, even, far, first_weight, first_late, first_last, second_weight, second_late, second_last, columns,
    branch_out, far_hidden, first_part, branch_part, hidden,
):
    started, joined = borders()
    bias, gain, last_bias = columns[0], columns[1], columns[2]

    def act(frame, row):
        if row < 0:
            return far[frame - 4, -1 - row]
        if row > 3:
            return even[frame, 5 - row]
        return earlier[frame, row] if frame < 4 else own[frame - 4, row]

    def inner(frame, row):
        return hidden[frame, row - 1]

    for frame in range(6):
        for row in (1, 3):
            pair = products(
                first_weight[...], window(act, frame, range(row - 1, row + 2)), window(act, frame, range(row, row + 3))
            )
            for step, sums in enumerate(pair):
                result = activation(sums + bias, gain)
                if frame < 2:
                    result = jnp.where(started, result, 0.0)
                hidden[frame, row - 1 + step] = result.astype(BF16)
    for frame in range(4):
        pair = products(
            second_weight[...], window(inner, frame, range(1, 4)), window(inner, frame, range(2, 5))
        )
        for step, sums in enumerate(pair):
            branch_out[frame, step] = sums + last_bias

    for frame in (4, 5):
        pair = products(first_weight[...], window(act, frame, (-2, -1, 0)), window(act, frame, (-1, 0, 1)))
        for step, sums in enumerate(pair):
            result = activation(sums + bias, gain)
            if step == 0:
                result = jnp.where(joined, result, 0.0)
            far_hidden[frame - 4, step] = result.astype(BF16)
    for frame in (0, 2):
        for part, cell, base, weights, row in (
            (first_part, act, bias, (first_last, first_late), 0),
            (branch_part, inner, last_bias, (second_last, second_late), 1),
        ):
            for step, weight in enumerate(weights):
                rows = (row,) if step == 0 else (row, row + 1)
                pair = products(weight[...], window(cell, frame, rows), window(cell, frame + 1, rows))
                for later, sums in enumerate(pair):
                    part[frame + later, step] = sums + base


def far_kernel(
    features, far, far_earlier, far_hidden, near_branch, first_part, branch_part, first_weight, second_weight, columns,
    encoded, hidden, total,
):
    started, joined = borders()
    gain = columns[1]

    def act(frame, row):
        return far_earlier[frame, -1 - row] if frame < 4 else far[frame - 4, -1 - row]

    def outer(frame, row):
        return hidden[frame, row + 1] if frame < 4 else far_hidden[frame - 4, row + 1]

    for frame in (0, 2):
        for step, rows in ((0, (-2, -1)), (1, (-1,))):
            weight = first_weight[:, : len(rows) * 3 * C]
            pair = products(weight, window(act, frame, rows), window(act, frame + 1, rows))
            for later, sums in enumerate(pair):
                result = activation(sums + first_part[frame + later, step], gain)
                keep = None
                if frame == 0:
                    keep = jnp.logical_and(started, joined) if step == 0 else started
                elif step == 0:
                    keep = joined
                if keep is not None:
                    result = jnp.where(keep, result, 0.0)
                hidden[frame + later, step] = result.astype(BF16)
    for frame in range(4):
        for step in range(2):
            total[pl.ds(frame * 4 + natural(step + 2), C, stride=16), :] = near_branch[frame, step]
    for frame in (0, 2):
        for step, rows in ((0, (-1, 0)), (1, (0,))):
            weight = second_weight[:, : len(rows) * 3 * C]
            pair = products(weight, window(outer, frame, rows), window(outer, frame + 1, rows))
            for later, sums in enumerate(pair):
                place = (frame + later) * 4 + natural(step)
                total[pl.ds(place, C, stride=16), :] = sums + branch_part[frame + later, step]

    encoded[...] = (features[...].astype(F32) + total[...]).astype(BF16)


def shape(*dims, dtype=BF16):
    return jax.ShapeDtypeStruct(dims, dtype)


def call(kernel, out_shape, scratch, inputs, **kwargs):
    many = isinstance(out_shape, (list, tuple))
    return pl.pallas_call(
        kernel,
        out_shape=out_shape,
        in_specs=[VMEM] * len(inputs),
        out_specs=[VMEM] * len(out_shape) if many else VMEM,
        scratch_shapes=scratch,
        compiler_params=PARAMS,
        **kwargs,
    )(*inputs)


def held(array, flops):
    return pl.pallas_call(
        lambda source, target: None,
        out_shape=jax.ShapeDtypeStruct(array.shape, array.dtype),
        in_specs=[pl.BlockSpec(memory_space=pl.ANY)],
        out_specs=pl.BlockSpec(memory_space=pl.ANY),
        input_output_aliases={0: 0},
        compiler_params=pltpu.CompilerParams(vmem_limit_bytes=1 << 20),
        cost_estimate=pl.CostEstimate(flops=flops, bytes_accessed=0, transcendentals=0),
    )(array)


def swap_pairs(first, count):
    edges = [(i, i + 1) for i in range(first, count - 1, 2)]
    return edges + [(b, a) for a, b in edges]


def local(features, first_gain, first_weight, first_bias, second_gain, second_weight, second_bias):
    height, times = lax.axis_size("height"), lax.axis_size("tm")
    later = [(i, i + 1) for i in range(times - 1)]
    flat = features.reshape(C * 16, W)
    rows = [v.reshape(1, C) for v in (first_bias, second_gain, second_bias)]

    edge, act, sent = pl.pallas_call(
        first_act_kernel,
        out_shape=[shape(4, 2, C, W), shape(4, 4, C, W), shape(4, 4, C, W)],
        in_specs=[pl.BlockSpec(memory_space=pltpu.HBM)] * 2,
        out_specs=[VMEM] * 3,
        scratch_shapes=[
            pltpu.VMEM((C * 16, W), BF16), pltpu.VMEM((1, C), F32), pltpu.VMEM((C * 16, W), F32),
            pltpu.SemaphoreType.DMA((2,)),
        ],
        compiler_params=PARAMS,
    )(*(pltpu.with_memory_space_constraint(v, pltpu.HBM) for v in (flat, first_gain.reshape(1, C))))
    far = lax.ppermute(edge, "height", swap_pairs(1, height))
    prepared = call(
        weight_kernel,
        [shape(3 * C, width * C) for width in (9, 6, 3)] * 2 + [shape(3, C, W, dtype=F32)], [],
        (first_weight, second_weight, *rows),
        cost_estimate=pl.CostEstimate(flops=1 << 35, bytes_accessed=1 << 21, transcendentals=0),
    )
    earlier = lax.ppermute(held(sent, 1 << 33), "tm", later)
    both = jnp.concatenate([earlier[:, 2:4], act[:, 2:4]], axis=0)
    both, prepared = lax.optimization_barrier((both, prepared))
    even = lax.ppermute(both, "height", swap_pairs(0, height))
    far = held(far, 1 << 33)
    far_earlier = lax.ppermute(far, "tm", later)
    near_branch, far_hidden, first_part, branch_part = call(
        near_kernel,
        [shape(4, 2, C, W, dtype=F32), shape(2, 2, C, W), shape(4, 2, C, W, dtype=F32), shape(4, 2, C, W, dtype=F32)],
        [pltpu.VMEM((6, 4, C, W), BF16)],
        (act, earlier, even, far, *prepared),
        cost_estimate=pl.CostEstimate(flops=40 * W * C * TAPS * 6, bytes_accessed=1 << 21, transcendentals=0),
    )
    encoded = call(
        far_kernel, shape(C * 16, W),
        [pltpu.VMEM((4, 2, C, W), BF16), pltpu.VMEM((C * 16, W), F32)],
        (flat, far, far_earlier, far_hidden, near_branch, first_part, branch_part, prepared[0], prepared[3], prepared[6]),
        cost_estimate=pl.CostEstimate(flops=8 * W * C * TAPS * 6, bytes_accessed=1 << 21, transcendentals=0),
    )
    return encoded.reshape(features.shape)


def solution(mesh):
    return jax.shard_map(
        local,
        mesh=mesh,
        in_specs=(P(None, "tm", "height", None), P(), P(), P(), P(), P(), P()),
        out_specs=P(None, "tm", "height", None),
        check_vma=False,
    )
```

time: 47.5 us -> 41.6 us (0.88)
  the two profiles are of different devices: /device:TPU:191 before, /device:TPU:448 now
where the time goes in v2:
time: 41.6 us; the launch traced here: 41.4 us
  starting transfers between devices  17.2 us (41%)
  waiting for transfers between devices  12.2 us (29%)
  Pallas kernels  11.2 us (27%)
  local copies, waits for them, and re-layouts  0.69 us (2%)
    ppermute x1, waiting for transfers between devices, local(): far = lax.ppermute(edge, 'height', swap_pairs(1, height))  10.5 us
    ppermute x1, starting transfers between devices, local(): far = lax.ppermute(edge, 'height', swap_pairs(1, height))  10.1 us
    pallas_call x3, Pallas kernels, call(): pl.pallas_call(kernel, out_shape=out_shape, in_specs=[VMEM] * len(inputs)...  9.57 us
    ppermute x1, starting transfers between devices, local(): earlier = lax.ppermute(held(sent, 1 << 33), 'tm', later)  3.06 us
    ppermute x1, starting transfers between devices, local(): far_earlier = lax.ppermute(far, 'tm', later)  2.04 us
    ppermute x1, starting transfers between devices, local(): even = lax.ppermute(both, 'height', swap_pairs(0, height))  1.92 us
    ppermute x1, waiting for transfers between devices, local(): far_earlier = lax.ppermute(far, 'tm', later)  1.65 us
    pallas_call x1, Pallas kernels, local(): pl.pallas_call(first_act_kernel, out_shape=[shape(4, 2, C, W), shape(4, 4...  1.61 us
  transfers between devices with their start and end apart: 4, of which 2 were waited for; matrix products, arithmetic and copies ran while one was open for 0% of the time, Pallas kernels for 17%

profile of v2, /device:TPU:448, one launch (start us, length us, event | category | flops | bytes accessed | tf_op | source)
XLA Modules:
  0.0 41.4 jit_solution(14629818845485156876)
XLA Ops:
  0.0 1.6 %shard_map.73 = (bf16[4,2,96,128]{3,2,1,0:T(8,128)(2,1)S(1)}, bf16[4,4,96,128]{3,2,1,0:T(8,128)(2,1)S(1)}, bf16[4,4,96,128]{3,2,1,0:T(8,128)(2,1)S(1)}) custom-call(bf16[1536,128]{1,0:T(8,128)(2,1)} %bitcast.6, f32[1,96]{1,0:T(1,128)} %bitcast.11), custom_call_target="tpu_custom_call" | custom-call | tf_op jit(solution)/shard_map/pallas_call | solution.py:234
  1.6 0.0 copy-start.1
  1.6 0.0 copy-start.2
  1.6 3.1 %collective-permute-start.2 = (bf16[4,4,96,128]{3,2,1,0:T(8,128)(2,1)S(1)}, bf16[4,4,96,128]{3,2,1,0:T(8,128)(2,1)S(1)}, u32[]{:S(2)}, u32[]{:S(2)}) collective-permute-start(bf16[4,4,96,128]{3,2,1,0:T(8,128)(2,1)S(1)} %shard_map.75), channel_id=1, source_target_pairs={{0,64},{64,128},{128,192},{192,256},{256,320},{320,384},{384,448},... | collective-permute-start | bytes 1179656 | tf_op jit(solution)/shard_map/ppermute | solution.py:252
  4.7 10.1 %collective-permute-start = (bf16[4,2,96,128]{3,2,1,0:T(8,128)(2,1)S(1)}, bf16[4,2,96,128]{3,2,1,0:T(8,128)(2,1)S(1)}, u32[]{:S(2)}, u32[]{:S(2)}) collective-permute-start(bf16[4,2,96,128]{3,2,1,0:T(8,128)(2,1)S(1)} %get-tuple-element.27), channel_id=1, source_target_pairs={{1,2},{3,4},{5,6},{7,8},{9,10},{11,12},{13,14},{15,16},{17,18},{19... | collective-permute-start | bytes 589832 | tf_op jit(solution)/shard_map/ppermute | solution.py:245
  14.9 0.0 copy-start.3
  14.9 0.0 copy-start.4
  14.9 0.0 copy-start.5
  14.9 0.0 copy-done.1
  14.9 0.0 copy-done.2
  14.9 0.6 %copy-done.3 = f32[96]{0:T(128)S(1)} copy-done((f32[96]{0:T(128)S(1)}, f32[96]{0:T(128)}, u32[]{:S(2)}) %copy-start.3) | copy-done | bytes 408
  15.5 0.0 copy-done.4
  15.5 0.0 copy-done.5
  15.6 3.2 %shard_map.76 = (bf16[288,864]{1,0:T(8,128)(2,1)S(1)}, bf16[288,576]{1,0:T(8,128)(2,1)S(1)}, bf16[288,288]{1,0:T(8,128)(2,1)S(1)}, bf16[288,864]{1,0:T(8,128)(2,...) custom-call(bf16[96,2592]{1,0:T(8,128)(2,1)S(1)} %copy-done.1, ...), custom_call_target="tpu_custom_call" | custom-call | flops 34359738368 | bytes 2097152 | tf_op jit(solution)/shard_map/pallas_call | solution.py:200
  18.8 0.0 collective-permute-done.2.earlier
  18.9 1.9 %collective-permute-start.3 = (bf16[8,2,96,128]{3,2,1,0:T(8,128)(2,1)S(1)}, bf16[8,2,96,128]{3,2,1,0:T(8,128)(2,1)S(1)}, u32[]{:S(2)}, u32[]{:S(2)}) collective-permute-start(bf16[8,2,96,128]{3,2,1,0:T(8,128)(2,1)S(1)} %pad_maximum_fusion), channel_id=1, source_target_pairs={{0,1},{2,3},{4,5},{6,7},{8,9},{10,11},{12,13},{14,15},{16,17},{18,... | collective-permute-start | bytes 1179656 | tf_op jit(solution)/shard_map/ppermute | solution.py:255
  20.8 10.5 %collective-permute-done.source = bf16[4,2,96,128]{3,2,1,0:T(8,128)(2,1)S(1)} collective-permute-done((bf16[4,2,96,128]{3,2,1,0:T(8,128)(2,1)S(1)}, bf16[4,2,96,128]{3,2,1,0:T(8,128)(2,1)S(1)}, u32[]{:S(2)}, u32[]{:S(2)}) %collective-permute-start) | collective-permute-done | bytes 196640 | tf_op jit(solution)/shard_map/ppermute | solution.py:245
  31.3 0.0 copy-start
  31.3 2.0 %collective-permute-start.1 = (bf16[4,2,96,128]{3,2,1,0:T(8,128)(2,1)S(1)}, bf16[4,2,96,128]{3,2,1,0:T(8,128)(2,1)S(1)}, u32[]{:S(2)}, u32[]{:S(2)}) collective-permute-start(bf16[4,2,96,128]{3,2,1,0:T(8,128)(2,1)S(1)} %shard_map.74.far), channel_id=1, source_target_pairs={{0,64},{64,128},{128,192},{192,256},{256,320},{320,384},{384,448},... | collective-permute-start | bytes 589832 | tf_op jit(solution)/shard_map/ppermute | solution.py:257
  33.4 0.0 collective-permute-done.3.even
  33.4 4.0 %shard_map.77 = (f32[4,2,96,128]{3,2,1,0:T(8,128)S(1)}, bf16[2,2,96,128]{3,2,1,0:T(8,128)(2,1)S(1)}, f32[4,2,96,128]{3,2,1,0:T(8,128)S(1)}, f32[4,2,96,128]{3,2,1,0:T(8,128)S(1)}) custom-call(bf16[4,4,96,128]{3,2,1,0:T(8,128)(2,1)S(1)} %get-tuple-element.28.own, bf16[4,4,96,128]{3,2,1,0:T(8,128)(2,1)S(1)} %collective-permute-done.2.earlier, ...), custom_call_target="tpu_custom_call" | custom-call | flops 2548039680 | bytes 2097152 | tf_op jit(solution)/shard_map/pallas_call | solution.py:200
  37.4 1.6 %collective-permute-done.1.far_earlier = bf16[4,2,96,128]{3,2,1,0:T(8,128)(2,1)S(1)} collective-permute-done((bf16[4,2,96,128]{3,2,1,0:T(8,128)(2,1)S(1)}, bf16[4,2,96,128]{3,2,1,0:T(8,128)(2,1)S(1)}, u32[]{:S(2)}, u32[]{:S(2)}) %collective-permute-start.1) | collective-permute-done | bytes 196640 | tf_op jit(solution)/shard_map/ppermute | solution.py:257
  39.0 0.0 copy-done
  39.0 2.4 %shard_map.78 = bf16[1536,128]{1,0:T(8,128)(2,1)} custom-call(bf16[1536,128]{1,0:T(8,128)(2,1)S(1)} %bitcast.7, bf16[4,2,96,128]{3,2,1,0:T(8,128)(2,1)S(1)} %shard_map.74.far, bf16[4,2,96,128]{3,2,1,0:T(8,128)(2,1)S(1)} %collective-permute-done.1.far_earlier, bf16[2,2,96,128]{3,2,1,0:T(8,128)(2,1)S(1)} %get-tuple-element.45.far_hidden, ...), custom_call_target="tpu_custom_call" | custom-call | flops 509607936 | bytes 2097152 | tf_op jit(solution)/shard_map/pallas_call | solution.py:200
  (5 shorter events, 0.1 us)
Async XLA Ops:
  1.6 13.3 %copy-start.1 = (bf16[96,2592]{1,0:T(8,128)(2,1)S(1)}, bf16[96,2592]{1,0:T(8,128)(2,1)}, u32[]{:S(2)}) copy-start(bf16[96,2592]{1,0:T(8,128)(2,1)} %first.1) | copy-start | bytes 1492996
  1.6 13.3 %copy-start.2 = (bf16[96,2592]{1,0:T(8,128)(2,1)S(1)}, bf16[96,2592]{1,0:T(8,128)(2,1)}, u32[]{:S(2)}) copy-start(bf16[96,2592]{1,0:T(8,128)(2,1)} %second.1) | copy-start | bytes 1492996
  1.6 17.2 %collective-permute-start.2 = (bf16[4,4,96,128]{3,2,1,0:T(8,128)(2,1)S(1)}, bf16[4,4,96,128]{3,2,1,0:T(8,128)(2,1)S(1)}, u32[]{:S(2)}, u32[]{:S(2)}) collective-permute-start(bf16[4,4,96,128]{3,2,1,0:T(8,128)(2,1)S(1)} %shard_map.75), channel_id=1, source_target_pairs={{0,64},{64,128},{128,192},{192,256},{256,320},{320,384},{384,448},... | collective-permute-start | bytes 1179656 | tf_op jit(solution)/shard_map/ppermute | solution.py:252
  4.7 26.6 %collective-permute-start = (bf16[4,2,96,128]{3,2,1,0:T(8,128)(2,1)S(1)}, bf16[4,2,96,128]{3,2,1,0:T(8,128)(2,1)S(1)}, u32[]{:S(2)}, u32[]{:S(2)}) collective-permute-start(bf16[4,2,96,128]{3,2,1,0:T(8,128)(2,1)S(1)} %get-tuple-element.27), channel_id=1, source_target_pairs={{1,2},{3,4},{5,6},{7,8},{9,10},{11,12},{13,14},{15,16},{17,18},{19... | collective-permute-start | bytes 589832 | tf_op jit(solution)/shard_map/ppermute | solution.py:245
  14.9 0.7 %copy-start.3 = (f32[96]{0:T(128)S(1)}, f32[96]{0:T(128)}, u32[]{:S(2)}) copy-start(f32[96]{0:T(128)} %param.10) | copy-start | bytes 1156
  14.9 0.7 %copy-start.4 = (f32[96]{0:T(128)S(1)}, f32[96]{0:T(128)}, u32[]{:S(2)}) copy-start(f32[96]{0:T(128)} %param.11) | copy-start | bytes 1156
  14.9 0.7 %copy-start.5 = (f32[96]{0:T(128)S(1)}, f32[96]{0:T(128)}, u32[]{:S(2)}) copy-start(f32[96]{0:T(128)} %param.13) | copy-start | bytes 1156
  18.9 14.5 %collective-permute-start.3 = (bf16[8,2,96,128]{3,2,1,0:T(8,128)(2,1)S(1)}, bf16[8,2,96,128]{3,2,1,0:T(8,128)(2,1)S(1)}, u32[]{:S(2)}, u32[]{:S(2)}) collective-permute-start(bf16[8,2,96,128]{3,2,1,0:T(8,128)(2,1)S(1)} %pad_maximum_fusion), channel_id=1, source_target_pairs={{0,1},{2,3},{4,5},{6,7},{8,9},{10,11},{12,13},{14,15},{16,17},{18,... | collective-permute-start | bytes 1179656 | tf_op jit(solution)/shard_map/ppermute | solution.py:255
  31.3 7.7 %copy-start = (bf16[96,4,4,128]{3,2,1,0:T(4,128)(2,1)S(1)}, bf16[96,4,4,128]{3,2,1,0:T(4,128)(2,1)}, u32[]{:S(2)}) copy-start(bf16[96,4,4,128]{3,2,1,0:T(4,128)(2,1)} %param.7) | copy-start | bytes 1179652
  31.3 7.7 %collective-permute-start.1 = (bf16[4,2,96,128]{3,2,1,0:T(8,128)(2,1)S(1)}, bf16[4,2,96,128]{3,2,1,0:T(8,128)(2,1)S(1)}, u32[]{:S(2)}, u32[]{:S(2)}) collective-permute-start(bf16[4,2,96,128]{3,2,1,0:T(8,128)(2,1)S(1)} %shard_map.74.far), channel_id=1, source_target_pairs={{0,64},{64,128},{128,192},{192,256},{256,320},{320,384},{384,448},... | collective-permute-start | bytes 589832 | tf_op jit(solution)/shard_map/ppermute | solution.py:257

commit v3 on v2

--- a/solution.py
+++ b/solution.py
@@ -10,6 +10,7 @@
 C = 96
 W = 128
 TAPS = 9 * C
+TURNS = {1: 1, 3: 1, 6: 1, 4: 2}
 BF16 = jnp.bfloat16
 F32 = jnp.float32
 VMEM = pl.BlockSpec(memory_space=pltpu.VMEM)
@@ -31,7 +32,7 @@
     return row + lax.rem(lax.axis_index("height"), 2) * (3 - 2 * row)
 
 
-def first_act_kernel(features_in, gain_in, edge, act, sent, features, gain_row, wide, arrived):
+def first_act_kernel(features_in, gain_in, act, features, gain_row, wide, arrived):
     copies = [
         pltpu.make_async_copy(features_in, features, arrived.at[0]),
         pltpu.make_async_copy(gain_in, gain_row, arrived.at[1]),
@@ -47,8 +48,6 @@
             values = wide[pl.ds(frame * 4 + row, C, stride=16), :]
             result = activation(values, gain).astype(BF16)
             act[frame, natural(row)] = result
-    edge[...] = act[:, 0:2]
-    sent[...] = act[...]
 
 
 def weight_kernel(first, second, first_bias, second_gain, second_bias, *targets):
@@ -56,22 +55,25 @@
     for step, row in enumerate((first_bias, second_gain, second_bias)):
         columns[step] = jnp.broadcast_to(column(row[...]), (C, W))
     reversed_rows = lax.rem(lax.axis_index("height"), 2) == 1
-    for source, (whole, late, last) in ((first, targets[0:3]), (second, targets[3:6])):
-        for row_tap in range(3):
-            for time_tap in range(3):
-                place = (row_tap * 3 + time_tap) * C
-                for tap in range(3):
-                    offset = ((time_tap * 3 + row_tap) * 3 + tap) * C
-                    mirrored = ((time_tap * 3 + 2 - row_tap) * 3 + tap) * C
-                    block = jnp.where(
-                        reversed_rows, source[:, mirrored : mirrored + C], source[:, offset : offset + C]
-                    )
-                    lines = slice(tap * C, (tap + 1) * C)
-                    whole[lines, place : place + C] = block
-                    if row_tap >= 1:
-                        late[lines, place - 3 * C : place - 2 * C] = block
-                    if row_tap == 2:
-                        last[lines, place - 6 * C : place - 5 * C] = block
+
+    def arrange(mirrored):
+        for source, (whole, late, last) in ((first, targets[0:3]), (second, targets[3:6])):
+            for row_tap in range(3):
+                for time_tap in range(3):
+                    place = (row_tap * 3 + time_tap) * C
+                    source_row = 2 - row_tap if mirrored else row_tap
+                    for tap in range(3):
+                        offset = ((time_tap * 3 + source_row) * 3 + tap) * C
+                        block = source[:, offset : offset + C]
+                        lines = slice(tap * C, (tap + 1) * C)
+                        whole[lines, place : place + C] = block
+                        if row_tap >= 1:
+                            late[lines, place - 3 * C : place - 2 * C] = block
+                        if row_tap == 2:
+                            last[lines, place - 6 * C : place - 5 * C] = block
+
+    pl.when(reversed_rows)(lambda: arrange(True))
+    pl.when(jnp.logical_not(reversed_rows))(lambda: arrange(False))
 
 
 def products(weight, left, right):
@@ -97,18 +99,14 @@
     return lax.axis_index("tm") > 0, jnp.logical_not(outer)
 
 
-def near_kernel(
-    own, earlier, even, far, first_weight, first_late, first_last, second_weight, second_late, second_last, columns,
-    branch_out, far_hidden, first_part, branch_part, hidden,
-):
-    started, joined = borders()
+def near_kernel(own, earlier, even, first_weight, second_weight, columns, near_hidden, branch_out, hidden):
+    started, _ = borders()
     bias, gain, last_bias = columns[0], columns[1], columns[2]
+    partner = 1 - lax.rem(lax.axis_index("height"), 2)
 
     def act(frame, row):
-        if row < 0:
-            return far[frame - 4, -1 - row]
         if row > 3:
-            return even[frame, 5 - row]
+            return even[partner, frame, 5 - row]
         return earlier[frame, row] if frame < 4 else own[frame - 4, row]
 
     def inner(frame, row):
@@ -124,12 +122,30 @@
                 if frame < 2:
                     result = jnp.where(started, result, 0.0)
                 hidden[frame, row - 1 + step] = result.astype(BF16)
+                if row == 1:
+                    near_hidden[frame, step] = result.astype(BF16)
     for frame in range(4):
         pair = products(
             second_weight[...], window(inner, frame, range(1, 4)), window(inner, frame, range(2, 5))
         )
         for step, sums in enumerate(pair):
             branch_out[frame, step] = sums + last_bias
+
+
+def partial_kernel(
+    own, earlier, far, near_hidden, first_weight, first_late, first_last, second_late, second_last, columns, _,
+    far_hidden, first_part, branch_part,
+):
+    _, joined = borders()
+    bias, gain, last_bias = columns[0], columns[1], columns[2]
+
+    def act(frame, row):
+        if row < 0:
+            return far[frame - 4, -1 - row]
+        return earlier[frame, row] if frame < 4 else own[frame - 4, row]
+
+    def inner(frame, row):
+        return near_hidden[frame, row - 1]
 
     for frame in (4, 5):
         pair = products(first_weight[...], window(act, frame, (-2, -1, 0)), window(act, frame, (-1, 0, 1)))
@@ -151,14 +167,16 @@
 
 
 def far_kernel(
-    features, far, far_earlier, far_hidden, near_branch, first_part, branch_part, first_weight, second_weight, columns,
+    features, far, corner, second_corner, third_corner, far_hidden, near_branch, first_part, branch_part, first_weight, second_weight, columns,
     encoded, hidden, total,
 ):
     started, joined = borders()
     gain = columns[1]
 
     def act(frame, row):
-        return far_earlier[frame, -1 - row] if frame < 4 else far[frame - 4, -1 - row]
+        if frame < 4:
+            return corner[frame, -1 - row] + second_corner[frame, -1 - row] + third_corner[frame, -1 - row]
+        return far[frame - 4, -1 - row]
 
     def outer(frame, row):
         return hidden[frame, row + 1] if frame < 4 else far_hidden[frame - 4, row + 1]
@@ -208,21 +226,35 @@
     )(*inputs)
 
 
-def held(array, flops):
+def held(array, flops, *others):
     return pl.pallas_call(
-        lambda source, target: None,
-        out_shape=jax.ShapeDtypeStruct(array.shape, array.dtype),
-        in_specs=[pl.BlockSpec(memory_space=pl.ANY)],
+        lambda *refs: None,
+        out_shape=shape(*array.shape),
+        in_specs=[pl.BlockSpec(memory_space=pl.ANY)] * (1 + len(others)),
         out_specs=pl.BlockSpec(memory_space=pl.ANY),
         input_output_aliases={0: 0},
         compiler_params=pltpu.CompilerParams(vmem_limit_bytes=1 << 20),
         cost_estimate=pl.CostEstimate(flops=flops, bytes_accessed=0, transcendentals=0),
-    )(array)
+    )(array, *others)
 
 
 def swap_pairs(first, count):
     edges = [(i, i + 1) for i in range(first, count - 1, 2)]
     return edges + [(b, a) for a, b in edges]
+
+
+def routes(times, height):
+    middle = (height // 2 - 1, height // 2)
+    crossing, corner = [[], [], []], [[], [], []]
+    for time in range(times):
+        for a, b in swap_pairs(1, height):
+            turn = TURNS.get(time, 0) if a in middle and b in middle else 0
+            crossing[turn].append((time * height + a, time * height + b))
+        for place in range(height):
+            turn = TURNS.get(time, 0) if place in middle else 0
+            if time + 1 < times:
+                corner[turn].append((time * height + place, (time + 1) * height + place))
+    return crossing, corner
 
 
 def local(features, first_gain, first_weight, first_bias, second_gain, second_weight, second_bias):
@@ -231,41 +263,48 @@
     flat = features.reshape(C * 16, W)
     rows = [v.reshape(1, C) for v in (first_bias, second_gain, second_bias)]
 
-    edge, act, sent = pl.pallas_call(
+    act = pl.pallas_call(
         first_act_kernel,
-        out_shape=[shape(4, 2, C, W), shape(4, 4, C, W), shape(4, 4, C, W)],
+        out_shape=shape(4, 4, C, W),
         in_specs=[pl.BlockSpec(memory_space=pltpu.HBM)] * 2,
-        out_specs=[VMEM] * 3,
+        out_specs=VMEM,
         scratch_shapes=[
             pltpu.VMEM((C * 16, W), BF16), pltpu.VMEM((1, C), F32), pltpu.VMEM((C * 16, W), F32),
             pltpu.SemaphoreType.DMA((2,)),
         ],
         compiler_params=PARAMS,
     )(*(pltpu.with_memory_space_constraint(v, pltpu.HBM) for v in (flat, first_gain.reshape(1, C))))
-    far = lax.ppermute(edge, "height", swap_pairs(1, height))
+    edge = act[:, 0:2]
+    crossing, corner = routes(times, height)
+    fars = [lax.ppermute(edge, ("tm", "height"), pairs) for pairs in crossing]
     prepared = call(
         weight_kernel,
         [shape(3 * C, width * C) for width in (9, 6, 3)] * 2 + [shape(3, C, W, dtype=F32)], [],
         (first_weight, second_weight, *rows),
-        cost_estimate=pl.CostEstimate(flops=1 << 35, bytes_accessed=1 << 21, transcendentals=0),
-    )
-    earlier = lax.ppermute(held(sent, 1 << 33), "tm", later)
+        cost_estimate=pl.CostEstimate(flops=1 << 27, bytes_accessed=1 << 21, transcendentals=0),
+    )
+    first, first_late, first_last, second, second_late, second_last, columns = prepared
+    earlier = lax.ppermute(act, "tm", later)
     both = jnp.concatenate([earlier[:, 2:4], act[:, 2:4]], axis=0)
-    both, prepared = lax.optimization_barrier((both, prepared))
-    even = lax.ppermute(both, "height", swap_pairs(0, height))
-    far = held(far, 1 << 33)
-    far_earlier = lax.ppermute(far, "tm", later)
-    near_branch, far_hidden, first_part, branch_part = call(
-        near_kernel,
-        [shape(4, 2, C, W, dtype=F32), shape(2, 2, C, W), shape(4, 2, C, W, dtype=F32), shape(4, 2, C, W, dtype=F32)],
-        [pltpu.VMEM((6, 4, C, W), BF16)],
-        (act, earlier, even, far, *prepared),
-        cost_estimate=pl.CostEstimate(flops=40 * W * C * TAPS * 6, bytes_accessed=1 << 21, transcendentals=0),
+    even = lax.all_gather(both, "height", axis_index_groups=[[i, i + 1] for i in range(0, height, 2)])
+    near_hidden, near_branch = call(
+        near_kernel, [shape(6, 2, C, W), shape(4, 2, C, W, dtype=F32)], [pltpu.VMEM((6, 4, C, W), BF16)],
+        (act, earlier, even, first, second, columns),
+        cost_estimate=pl.CostEstimate(flops=1 << 20, bytes_accessed=1 << 10, transcendentals=0),
+    )
+    fars = [held(far, 1 << 33, near_hidden) for far in fars]
+    corners = [lax.ppermute(far, ("tm", "height"), pairs) for far, pairs in zip(fars, corner)]
+    far = fars[0] + fars[1] + fars[2]
+    far_hidden, first_part, branch_part = call(
+        partial_kernel,
+        [shape(2, 2, C, W), shape(4, 2, C, W, dtype=F32), shape(4, 2, C, W, dtype=F32)], [],
+        (act, earlier, far, near_hidden, first, first_late, first_last, second_late, second_last, columns, corners[0]),
+        cost_estimate=pl.CostEstimate(flops=1 << 30, bytes_accessed=1 << 21, transcendentals=0),
     )
     encoded = call(
         far_kernel, shape(C * 16, W),
         [pltpu.VMEM((4, 2, C, W), BF16), pltpu.VMEM((C * 16, W), F32)],
-        (flat, far, far_earlier, far_hidden, near_branch, first_part, branch_part, prepared[0], prepared[3], prepared[6]),
+        (flat, far, *corners, far_hidden, near_branch, first_part, branch_part, first, second, columns),
         cost_estimate=pl.CostEstimate(flops=8 * W * C * TAPS * 6, bytes_accessed=1 << 21, transcendentals=0),
     )
     return encoded.reshape(features.shape)

time: 41.6 us -> 40.4 us (0.971)
  the two profiles are of different devices: /device:TPU:448 before, /device:TPU:62 now
where the time goes in v3:
time: 40.4 us; the launch traced here: 40.2 us
  starting transfers between devices  11.5 us (28%)
  blocking collectives  9.93 us (25%)
  Pallas kernels  9.26 us (23%)
  waiting for transfers between devices  8.51 us (21%)
  local copies, waits for them, and re-layouts  0.7 us (2%)
    all_gather x1, blocking collectives, local(): lax.all_gather(both, 'height', axis_index_groups=[[i, i + 1] for i in ran...  9.93 us
    pallas_call x4, Pallas kernels, call(): pl.pallas_call(kernel, out_shape=out_shape, in_specs=[VMEM] * len(inputs)...  7.64 us
    ppermute x3, waiting for transfers between devices, local(): lax.ppermute(far, ('tm', 'height'), pairs)  4.7 us
    ppermute x3, starting transfers between devices, local(): lax.ppermute(far, ('tm', 'height'), pairs)  4.27 us
    ppermute x1, starting transfers between devices, local(): earlier = lax.ppermute(act, 'tm', later)  3.96 us
    ppermute x1, waiting for transfers between devices, local(): earlier = lax.ppermute(act, 'tm', later)  3.8 us
    ppermute x3, starting transfers between devices, local(): fars = [lax.ppermute(edge, ('tm', 'height'), pairs) for pairs in crossing]  3.27 us
    pallas_call x1, Pallas kernels, local(): pl.pallas_call(first_act_kernel, out_shape=shape(4, 4, C, W), in_specs=[p...  1.6 us
  transfers between devices with their start and end apart: 7, of which 2 were waited for; matrix products, arithmetic and copies ran while one was open for 0% of the time, Pallas kernels for 13%

profile of v3, /device:TPU:62, one launch (start us, length us, event | category | flops | bytes accessed | tf_op | source)
XLA Modules:
  0.0 40.2 jit_solution(3538017283282891920)
XLA Ops:
  0.0 0.0 copy-start.2
  0.0 1.6 %shard_map.73.own = bf16[4,4,96,128]{3,2,1,0:T(8,128)(2,1)S(1)} custom-call(bf16[1536,128]{1,0:T(8,128)(2,1)} %bitcast.8, f32[1,96]{1,0:T(1,128)} %bitcast.13), custom_call_target="tpu_custom_call" | custom-call | tf_op jit(solution)/shard_map/pallas_call | solution.py:266
  1.6 0.0 copy-start.1
  1.6 4.0 %collective-permute-start.1 = (bf16[4,4,96,128]{3,2,1,0:T(8,128)(2,1)S(1)}, bf16[4,4,96,128]{3,2,1,0:T(8,128)(2,1)S(1)}, u32[]{:S(2)}, u32[]{:S(2)}) collective-permute-start(bf16[4,4,96,128]{3,2,1,0:T(8,128)(2,1)S(1)} %shard_map.73.own), channel_id=1, source_target_pairs={{0,64},{64,128},{128,192},{192,256},{256,320},{320,384},{384,448},... | collective-permute-start | bytes 1179656 | tf_op jit(solution)/shard_map/ppermute | solution.py:287
  5.6 0.7 %collective-permute-start.3 = (bf16[4,2,96,128]{3,2,1,0:T(8,128)(2,1)S(1)}, bf16[4,2,96,128]{3,2,1,0:T(8,128)(2,1)S(1)}, u32[]{:S(2)}, u32[]{:S(2)}) collective-permute-start(bf16[4,2,96,128]{3,2,1,0:T(8,128)(2,1)S(1)} %get-tuple-element.30), channel_id=1, source_target_pairs={{287,288},{288,287}} | collective-permute-start | bytes 589832 | tf_op jit(solution)/shard_map/ppermute | solution.py:279
  6.3 0.7 %collective-permute-start.2 = (bf16[4,2,96,128]{3,2,1,0:T(8,128)(2,1)S(1)}, bf16[4,2,96,128]{3,2,1,0:T(8,128)(2,1)S(1)}, u32[]{:S(2)}, u32[]{:S(2)}) collective-permute-start(bf16[4,2,96,128]{3,2,1,0:T(8,128)(2,1)S(1)} %get-tuple-element.30), channel_id=1, source_target_pairs={{95,96},{96,95},{223,224},{224,223},{415,416},{416,415}} | collective-permute-start | bytes 589832 | tf_op jit(solution)/shard_map/ppermute | solution.py:279
  7.0 1.9 %collective-permute-start = (bf16[4,2,96,128]{3,2,1,0:T(8,128)(2,1)S(1)}, bf16[4,2,96,128]{3,2,1,0:T(8,128)(2,1)S(1)}, u32[]{:S(2)}, u32[]{:S(2)}) collective-permute-start(bf16[4,2,96,128]{3,2,1,0:T(8,128)(2,1)S(1)} %get-tuple-element.30), channel_id=1, source_target_pairs={{1,2},{3,4},{5,6},{7,8},{9,10},{11,12},{13,14},{15,16},{17,18},{19... | collective-permute-start | bytes 589832 | tf_op jit(solution)/shard_map/ppermute | solution.py:279
  8.9 0.0 copy-start.3
  8.9 0.0 copy-start.4
  8.9 0.0 copy-start.5
  9.0 0.0 copy-done.2
  9.0 0.0 copy-done.1
  9.0 0.6 %copy-done.3 = f32[96]{0:T(128)S(1)} copy-done((f32[96]{0:T(128)S(1)}, f32[96]{0:T(128)}, u32[]{:S(2)}) %copy-start.3) | copy-done | bytes 408
  9.6 0.0 copy-done.4
  9.6 0.0 copy-done.5
  9.6 1.1 %shard_map.74 = (bf16[288,864]{1,0:T(8,128)(2,1)S(1)}, bf16[288,576]{1,0:T(8,128)(2,1)S(1)}, bf16[288,288]{1,0:T(8,128)(2,1)S(1)}, bf16[288,864]{1,0:T(8,128)(2,...) custom-call(bf16[96,2592]{1,0:T(8,128)(2,1)S(1)} %copy-done.1, ...), custom_call_target="tpu_custom_call" | custom-call | flops 134217728 | bytes 2097152 | tf_op jit(solution)/shard_map/pallas_call | solution.py:218
  10.7 3.8 %collective-permute-done.1.earlier = bf16[4,4,96,128]{3,2,1,0:T(8,128)(2,1)S(1)} collective-permute-done((bf16[4,4,96,128]{3,2,1,0:T(8,128)(2,1)S(1)}, bf16[4,4,96,128]{3,2,1,0:T(8,128)(2,1)S(1)}, u32[]{:S(2)}, u32[]{:S(2)}) %collective-permute-start.1) | collective-permute-done | bytes 393248 | tf_op jit(solution)/shard_map/ppermute | solution.py:287
  14.6 9.9 %all-gather = bf16[16,2,96,128]{3,2,1,0:T(8,128)(2,1)S(1)} all-gather(bf16[8,2,96,128]{3,2,1,0:T(8,128)(2,1)S(1)} %pad_maximum_fusion), channel_id=2, replica_groups={{0,1},{2,3},{4,5},{6,7},{8,9},{10,11},{12,13},{14,15},{16,17},{18,19},{..., dimensions={0}, use_global_device_ids=true | all-gather | bytes 1179648 | tf_op jit(solution)/shard_map/all_gather | solution.py:289
  24.5 2.8 %shard_map.75 = (bf16[6,2,96,128]{3,2,1,0:T(8,128)(2,1)S(1)}, f32[4,2,96,128]{3,2,1,0:T(8,128)S(1)}) custom-call(bf16[4,4,96,128]{3,2,1,0:T(8,128)(2,1)S(1)} %shard_map.73.own, bf16[4,4,96,128]{3,2,1,0:T(8,128)(2,1)S(1)} %collective-permute-done.1.earlier, bf16[2,8,2,96,128]{4,3,2,1,0:T(8,128)(2,1)S(1)} %bitcast.7, ...), custom_call_target="tpu_custom_call" | custom-call | flops 1048576 | bytes 1024 | tf_op jit(solution)/shard_map/pallas_call | solution.py:218
  27.3 0.0 collective-permute-done.refs_0_
  27.3 2.9 %collective-permute-start.4 = (bf16[4,2,96,128]{3,2,1,0:T(8,128)(2,1)S(1)}, bf16[4,2,96,128]{3,2,1,0:T(8,128)(2,1)S(1)}, u32[]{:S(2)}, u32[]{:S(2)}) collective-permute-start(bf16[4,2,96,128]{3,2,1,0:T(8,128)(2,1)S(1)} %shard_map.76), channel_id=1, source_target_pairs={{0,64},{1,65},{2,66},{3,67},{4,68},{5,69},{6,70},{7,71},{8,72},{9,... | collective-permute-start | bytes 589832 | tf_op jit(solution)/shard_map/ppermute | solution.py:296
  30.2 0.0 collective-permute-done.2.refs_0_
  30.3 0.7 %collective-permute-start.5 = (bf16[4,2,96,128]{3,2,1,0:T(8,128)(2,1)S(1)}, bf16[4,2,96,128]{3,2,1,0:T(8,128)(2,1)S(1)}, u32[]{:S(2)}, u32[]{:S(2)}) collective-permute-start(bf16[4,2,96,128]{3,2,1,0:T(8,128)(2,1)S(1)} %shard_map.77), channel_id=1, source_target_pairs={{95,159},{96,160},{223,287},{224,288},{415,479},{416,480}} | collective-permute-start | bytes 589832 | tf_op jit(solution)/shard_map/ppermute | solution.py:296
  30.9 0.0 collective-permute-done.3.refs_0_
  31.0 0.7 %collective-permute-start.6 = (bf16[4,2,96,128]{3,2,1,0:T(8,128)(2,1)S(1)}, bf16[4,2,96,128]{3,2,1,0:T(8,128)(2,1)S(1)}, u32[]{:S(2)}, u32[]{:S(2)}) collective-permute-start(bf16[4,2,96,128]{3,2,1,0:T(8,128)(2,1)S(1)} %shard_map.78), channel_id=1, source_target_pairs={{287,351},{288,352}} | collective-permute-start | bytes 589832 | tf_op jit(solution)/shard_map/ppermute | solution.py:296
  31.7 4.7 %collective-permute-done.4._.corner = bf16[4,2,96,128]{3,2,1,0:T(8,128)(2,1)S(1)} collective-permute-done((bf16[4,2,96,128]{3,2,1,0:T(8,128)(2,1)S(1)}, bf16[4,2,96,128]{3,2,1,0:T(8,128)(2,1)S(1)}, u32[]{:S(2)}, u32[]{:S(2)}) %collective-permute-start.4) | collective-permute-done | bytes 196640 | tf_op jit(solution)/shard_map/ppermute | solution.py:296
  36.4 0.0 copy-start
  36.4 1.4 %shard_map.79 = (bf16[2,2,96,128]{3,2,1,0:T(8,128)(2,1)S(1)}, f32[4,2,96,128]{3,2,1,0:T(8,128)S(1)}, f32[4,2,96,128]{3,2,1,0:T(8,128)S(1)}) custom-call(bf16[4,4,96,128]{3,2,1,0:T(8,128)(2,1)S(1)} %shard_map.73.own, bf16[4,4,96,128]{3,2,1,0:T(8,128)(2,1)S(1)} %collective-permute-done.1.earlier, bf16[4,2,96,128]{3,2,1,0:T(8,128)(2,1)S(1)} %add_add_fusion.far, ...), custom_call_target="tpu_custom_call" | custom-call | flops 1073741824 | bytes 2097152 | tf_op jit(solution)/shard_map/pallas_call | solution.py:218
  37.8 0.0 collective-permute-done.5.second_corner
  37.8 0.0 collective-permute-done.6.third_corner
  37.8 0.0 copy-done
  37.8 2.4 %shard_map.80 = bf16[1536,128]{1,0:T(8,128)(2,1)} custom-call(bf16[1536,128]{1,0:T(8,128)(2,1)S(1)} %bitcast.9, bf16[4,2,96,128]{3,2,1,0:T(8,128)(2,1)S(1)} %add_add_fusion.far, bf16[4,2,96,128]{3,2,1,0:T(8,128)(2,1)S(1)} %collective-permute-done.4._.corner, bf16[4,2,96,128]{3,2,1,0:T(8,128)(2,1)S(1)} %collective-permute-done.5.second_corner, ...), custom_call_target="tpu_custom_call" | custom-call | flops 509607936 | bytes 2097152 | tf_op jit(solution)/shard_map/pallas_call | solution.py:218
  (7 shorter events, 0.1 us)
Async XLA Ops:
  0.0 9.0 %copy-start.2 = (bf16[96,2592]{1,0:T(8,128)(2,1)S(1)}, bf16[96,2592]{1,0:T(8,128)(2,1)}, u32[]{:S(2)}) copy-start(bf16[96,2592]{1,0:T(8,128)(2,1)} %second.1) | copy-start | bytes 1492996
  1.6 7.4 %copy-start.1 = (bf16[96,2592]{1,0:T(8,128)(2,1)S(1)}, bf16[96,2592]{1,0:T(8,128)(2,1)}, u32[]{:S(2)}) copy-start(bf16[96,2592]{1,0:T(8,128)(2,1)} %first.1) | copy-start | bytes 1492996
  1.6 12.9 %collective-permute-start.1 = (bf16[4,4,96,128]{3,2,1,0:T(8,128)(2,1)S(1)}, bf16[4,4,96,128]{3,2,1,0:T(8,128)(2,1)S(1)}, u32[]{:S(2)}, u32[]{:S(2)}) collective-permute-start(bf16[4,4,96,128]{3,2,1,0:T(8,128)(2,1)S(1)} %shard_map.73.own), channel_id=1, source_target_pairs={{0,64},{64,128},{128,192},{192,256},{256,320},{320,384},{384,448},... | collective-permute-start | bytes 1179656 | tf_op jit(solution)/shard_map/ppermute | solution.py:287
  5.6 25.3 %collective-permute-start.3 = (bf16[4,2,96,128]{3,2,1,0:T(8,128)(2,1)S(1)}, bf16[4,2,96,128]{3,2,1,0:T(8,128)(2,1)S(1)}, u32[]{:S(2)}, u32[]{:S(2)}) collective-permute-start(bf16[4,2,96,128]{3,2,1,0:T(8,128)(2,1)S(1)} %get-tuple-element.30), channel_id=1, source_target_pairs={{287,288},{288,287}} | collective-permute-start | bytes 589832 | tf_op jit(solution)/shard_map/ppermute | solution.py:279
  6.3 23.9 %collective-permute-start.2 = (bf16[4,2,96,128]{3,2,1,0:T(8,128)(2,1)S(1)}, bf16[4,2,96,128]{3,2,1,0:T(8,128)(2,1)S(1)}, u32[]{:S(2)}, u32[]{:S(2)}) collective-permute-start(bf16[4,2,96,128]{3,2,1,0:T(8,128)(2,1)S(1)} %get-tuple-element.30), channel_id=1, source_target_pairs={{95,96},{96,95},{223,224},{224,223},{415,416},{416,415}} | collective-permute-start | bytes 589832 | tf_op jit(solution)/shard_map/ppermute | solution.py:279
  7.0 20.3 %collective-permute-start = (bf16[4,2,96,128]{3,2,1,0:T(8,128)(2,1)S(1)}, bf16[4,2,96,128]{3,2,1,0:T(8,128)(2,1)S(1)}, u32[]{:S(2)}, u32[]{:S(2)}) collective-permute-start(bf16[4,2,96,128]{3,2,1,0:T(8,128)(2,1)S(1)} %get-tuple-element.30), channel_id=1, source_target_pairs={{1,2},{3,4},{5,6},{7,8},{9,10},{11,12},{13,14},{15,16},{17,18},{19... | collective-permute-start | bytes 589832 | tf_op jit(solution)/shard_map/ppermute | solution.py:279
  8.9 0.7 %copy-start.3 = (f32[96]{0:T(128)S(1)}, f32[96]{0:T(128)}, u32[]{:S(2)}) copy-start(f32[96]{0:T(128)} %param.10) | copy-start | bytes 1156
  8.9 0.7 %copy-start.4 = (f32[96]{0:T(128)S(1)}, f32[96]{0:T(128)}, u32[]{:S(2)}) copy-start(f32[96]{0:T(128)} %param.11) | copy-start | bytes 1156
  8.9 0.7 %copy-start.5 = (f32[96]{0:T(128)S(1)}, f32[96]{0:T(128)}, u32[]{:S(2)}) copy-start(f32[96]{0:T(128)} %param.13) | copy-start | bytes 1156
  27.3 9.1 %collective-permute-start.4 = (bf16[4,2,96,128]{3,2,1,0:T(8,128)(2,1)S(1)}, bf16[4,2,96,128]{3,2,1,0:T(8,128)(2,1)S(1)}, u32[]{:S(2)}, u32[]{:S(2)}) collective-permute-start(bf16[4,2,96,128]{3,2,1,0:T(8,128)(2,1)S(1)} %shard_map.76), channel_id=1, source_target_pairs={{0,64},{1,65},{2,66},{3,67},{4,68},{5,69},{6,70},{7,71},{8,72},{9,... | collective-permute-start | bytes 589832 | tf_op jit(solution)/shard_map/ppermute | solution.py:296
  30.3 7.5 %collective-permute-start.5 = (bf16[4,2,96,128]{3,2,1,0:T(8,128)(2,1)S(1)}, bf16[4,2,96,128]{3,2,1,0:T(8,128)(2,1)S(1)}, u32[]{:S(2)}, u32[]{:S(2)}) collective-permute-start(bf16[4,2,96,128]{3,2,1,0:T(8,128)(2,1)S(1)} %shard_map.77), channel_id=1, source_target_pairs={{95,159},{96,160},{223,287},{224,288},{415,479},{416,480}} | collective-permute-start | bytes 589832 | tf_op jit(solution)/shard_map/ppermute | solution.py:296
  31.0 6.8 %collective-permute-start.6 = (bf16[4,2,96,128]{3,2,1,0:T(8,128)(2,1)S(1)}, bf16[4,2,96,128]{3,2,1,0:T(8,128)(2,1)S(1)}, u32[]{:S(2)}, u32[]{:S(2)}) collective-permute-start(bf16[4,2,96,128]{3,2,1,0:T(8,128)(2,1)S(1)} %shard_map.78), channel_id=1, source_target_pairs={{287,351},{288,352}} | collective-permute-start | bytes 589832 | tf_op jit(solution)/shard_map/ppermute | solution.py:296
  36.4 1.4 %copy-start = (bf16[96,4,4,128]{3,2,1,0:T(4,128)(2,1)S(1)}, bf16[96,4,4,128]{3,2,1,0:T(4,128)(2,1)}, u32[]{:S(2)}) copy-start(bf16[96,4,4,128]{3,2,1,0:T(4,128)(2,1)} %param.7) | copy-start | bytes 1179652

commit v4 on v3

--- a/solution.py
+++ b/solution.py
@@ -50,8 +50,9 @@
             act[frame, natural(row)] = result
 
 
-def weight_kernel(first, second, first_bias, second_gain, second_bias, *targets):
-    columns = targets[-1]
+def weight_kernel(first, second, first_bias, second_gain, second_bias, features, *targets):
+    columns, kept = targets[-2:]
+    kept[...] = features[...]
     for step, row in enumerate((first_bias, second_gain, second_bias)):
         columns[step] = jnp.broadcast_to(column(row[...]), (C, W))
     reversed_rows = lax.rem(lax.axis_index("height"), 2) == 1
@@ -133,7 +134,7 @@
 
 
 def partial_kernel(
-    own, earlier, far, near_hidden, first_weight, first_late, first_last, second_late, second_last, columns, _,
+    own, earlier, far, near_hidden, first_weight, first_late, first_last, second_late, second_last, columns,
     far_hidden, first_part, branch_part,
 ):
     _, joined = borders()
@@ -279,11 +280,11 @@
     fars = [lax.ppermute(edge, ("tm", "height"), pairs) for pairs in crossing]
     prepared = call(
         weight_kernel,
-        [shape(3 * C, width * C) for width in (9, 6, 3)] * 2 + [shape(3, C, W, dtype=F32)], [],
-        (first_weight, second_weight, *rows),
+        [shape(3 * C, width * C) for width in (9, 6, 3)] * 2 + [shape(3, C, W, dtype=F32), shape(C * 16, W)], [],
+        (first_weight, second_weight, *rows, flat),
         cost_estimate=pl.CostEstimate(flops=1 << 27, bytes_accessed=1 << 21, transcendentals=0),
     )
-    first, first_late, first_last, second, second_late, second_last, columns = prepared
+    first, first_late, first_last, second, second_late, second_last, columns, kept = prepared
     earlier = lax.ppermute(act, "tm", later)
     both = jnp.concatenate([earlier[:, 2:4], act[:, 2:4]], axis=0)
     even = lax.all_gather(both, "height", axis_index_groups=[[i, i + 1] for i in range(0, height, 2)])
@@ -292,19 +293,21 @@
         (act, earlier, even, first, second, columns),
         cost_estimate=pl.CostEstimate(flops=1 << 20, bytes_accessed=1 << 10, transcendentals=0),
     )
-    fars = [held(far, 1 << 33, near_hidden) for far in fars]
+    fars[0], fars[1] = (held(far, 1 << 33, near_hidden) for far in fars[:2])
+    fars[2] = held(fars[2], 1 << 33, near_hidden, fars[1])
     corners = [lax.ppermute(far, ("tm", "height"), pairs) for far, pairs in zip(fars, corner)]
-    far = fars[0] + fars[1] + fars[2]
+    corners[0] = held(corners[0], 1 << 28)
+    far = fars[0] + fars[2] + fars[1]
     far_hidden, first_part, branch_part = call(
         partial_kernel,
         [shape(2, 2, C, W), shape(4, 2, C, W, dtype=F32), shape(4, 2, C, W, dtype=F32)], [],
-        (act, earlier, far, near_hidden, first, first_late, first_last, second_late, second_last, columns, corners[0]),
+        (act, earlier, far, near_hidden, first, first_late, first_last, second_late, second_last, columns),
         cost_estimate=pl.CostEstimate(flops=1 << 30, bytes_accessed=1 << 21, transcendentals=0),
     )
     encoded = call(
         far_kernel, shape(C * 16, W),
         [pltpu.VMEM((4, 2, C, W), BF16), pltpu.VMEM((C * 16, W), F32)],
-        (flat, far, *corners, far_hidden, near_branch, first_part, branch_part, first, second, columns),
+        (kept, far, *corners, far_hidden, near_branch, first_part, branch_part, first, second, columns),
         cost_estimate=pl.CostEstimate(flops=8 * W * C * TAPS * 6, bytes_accessed=1 << 21, transcendentals=0),
     )
     return encoded.reshape(features.shape)

time: 40.4 us -> 40.1 us (level)
  the two profiles are of different devices: /device:TPU:62 before, /device:TPU:95 now
where the time goes in v4:
time: 40.1 us; the launch traced here: 39.8 us
  starting transfers between devices  21.4 us (53%)
  Pallas kernels  9.34 us (23%)
  waiting for transfers between devices  5.69 us (14%)
  blocking collectives  2.37 us (6%)
  local copies, waits for them, and re-layouts  0.69 us (2%)
    ppermute x3, starting transfers between devices, local(): fars = [lax.ppermute(edge, ('tm', 'height'), pairs) for pairs in crossing]  14.5 us
    pallas_call x4, Pallas kernels, call(): pl.pallas_call(kernel, out_shape=out_shape, in_specs=[VMEM] * len(inputs)...  7.7 us
    ppermute x1, starting transfers between devices, local(): earlier = lax.ppermute(act, 'tm', later)  3.68 us
    ppermute x3, starting transfers between devices, local(): lax.ppermute(far, ('tm', 'height'), pairs)  3.26 us
    ppermute x3, waiting for transfers between devices, local(): lax.ppermute(far, ('tm', 'height'), pairs)  2.98 us
    ppermute x3, waiting for transfers between devices, local(): fars = [lax.ppermute(edge, ('tm', 'height'), pairs) for pairs in crossing]  2.71 us
    all_gather x1, blocking collectives, local(): lax.all_gather(both, 'height', axis_index_groups=[[i, i + 1] for i in ran...  2.37 us
    pallas_call x1, Pallas kernels, local(): pl.pallas_call(first_act_kernel, out_shape=shape(4, 4, C, W), in_specs=[p...  1.63 us
  transfers between devices with their start and end apart: 7, of which 3 were waited for; matrix products, arithmetic and copies ran while one was open for 0% of the time, Pallas kernels for 13%

profile of v4, /device:TPU:95, one launch (start us, length us, event | category | flops | bytes accessed | tf_op | source)
XLA Modules:
  0.0 39.8 jit_solution(14044759910709304842)
XLA Ops:
  0.0 0.0 copy-start.1
  0.0 0.0 copy-start.2
  0.0 1.6 %shard_map.74.own = bf16[4,4,96,128]{3,2,1,0:T(8,128)(2,1)S(1)} custom-call(bf16[1536,128]{1,0:T(8,128)(2,1)} %bitcast.8, f32[1,96]{1,0:T(1,128)} %bitcast.13), custom_call_target="tpu_custom_call" | custom-call | tf_op jit(solution)/shard_map/pallas_call | solution.py:267
  1.6 0.0 copy-start
  1.7 3.7 %collective-permute-start.1 = (bf16[4,4,96,128]{3,2,1,0:T(8,128)(2,1)S(1)}, bf16[4,4,96,128]{3,2,1,0:T(8,128)(2,1)S(1)}, u32[]{:S(2)}, u32[]{:S(2)}) collective-permute-start(bf16[4,4,96,128]{3,2,1,0:T(8,128)(2,1)S(1)} %shard_map.74.own), channel_id=1, source_target_pairs={{0,64},{64,128},{128,192},{192,256},{256,320},{320,384},{384,448},... | collective-permute-start | bytes 1179656 | tf_op jit(solution)/shard_map/ppermute | solution.py:288
  5.4 0.7 %collective-permute-start.3 = (bf16[4,2,96,128]{3,2,1,0:T(8,128)(2,1)S(1)}, bf16[4,2,96,128]{3,2,1,0:T(8,128)(2,1)S(1)}, u32[]{:S(2)}, u32[]{:S(2)}) collective-permute-start(bf16[4,2,96,128]{3,2,1,0:T(8,128)(2,1)S(1)} %get-tuple-element.32), channel_id=1, source_target_pairs={{95,96},{96,95},{223,224},{224,223},{415,416},{416,415}} | collective-permute-start | bytes 589832 | tf_op jit(solution)/shard_map/ppermute | solution.py:280
  6.1 0.7 %collective-permute-start.2 = (bf16[4,2,96,128]{3,2,1,0:T(8,128)(2,1)S(1)}, bf16[4,2,96,128]{3,2,1,0:T(8,128)(2,1)S(1)}, u32[]{:S(2)}, u32[]{:S(2)}) collective-permute-start(bf16[4,2,96,128]{3,2,1,0:T(8,128)(2,1)S(1)} %get-tuple-element.32), channel_id=1, source_target_pairs={{287,288},{288,287}} | collective-permute-start | bytes 589832 | tf_op jit(solution)/shard_map/ppermute | solution.py:280
  6.7 13.2 %collective-permute-start = (bf16[4,2,96,128]{3,2,1,0:T(8,128)(2,1)S(1)}, bf16[4,2,96,128]{3,2,1,0:T(8,128)(2,1)S(1)}, u32[]{:S(2)}, u32[]{:S(2)}) collective-permute-start(bf16[4,2,96,128]{3,2,1,0:T(8,128)(2,1)S(1)} %get-tuple-element.32), channel_id=1, source_target_pairs={{1,2},{3,4},{5,6},{7,8},{9,10},{11,12},{13,14},{15,16},{17,18},{19... | collective-permute-start | bytes 589832 | tf_op jit(solution)/shard_map/ppermute | solution.py:280
  19.9 0.0 copy-start.3
  19.9 0.0 copy-start.4
  19.9 0.0 copy-start.5
  19.9 0.0 copy-done.1
  20.0 0.0 copy-done.2
  20.0 0.0 copy-done
  20.0 0.6 %copy-done.3 = f32[96]{0:T(128)S(1)} copy-done((f32[96]{0:T(128)S(1)}, f32[96]{0:T(128)}, u32[]{:S(2)}) %copy-start.3) | copy-done | bytes 408
  20.6 0.0 copy-done.4
  20.6 0.0 copy-done.5
  20.6 1.1 %shard_map.73 = (bf16[288,864]{1,0:T(8,128)(2,1)S(1)}, bf16[288,576]{1,0:T(8,128)(2,1)S(1)}, bf16[288,288]{1,0:T(8,128)(2,1)S(1)}, bf16[288,864]{1,0:T(8,128)(2,...) custom-call(bf16[96,2592]{1,0:T(8,128)(2,1)S(1)} %copy-done.1, ...), custom_call_target="tpu_custom_call" | custom-call | flops 134217728 | bytes 2097152 | tf_op jit(solution)/shard_map/pallas_call | solution.py:219
  21.7 0.0 collective-permute-done.1.earlier
  21.8 2.4 %all-gather = bf16[16,2,96,128]{3,2,1,0:T(8,128)(2,1)S(1)} all-gather(bf16[8,2,96,128]{3,2,1,0:T(8,128)(2,1)S(1)} %pad_maximum_fusion), channel_id=2, replica_groups={{0,1},{2,3},{4,5},{6,7},{8,9},{10,11},{12,13},{14,15},{16,17},{18,19},{..., dimensions={0}, use_global_device_ids=true | all-gather | bytes 1179648 | tf_op jit(solution)/shard_map/all_gather | solution.py:290
  24.2 2.8 %shard_map.75 = (bf16[6,2,96,128]{3,2,1,0:T(8,128)(2,1)S(1)}, f32[4,2,96,128]{3,2,1,0:T(8,128)S(1)}) custom-call(bf16[4,4,96,128]{3,2,1,0:T(8,128)(2,1)S(1)} %shard_map.74.own, bf16[4,4,96,128]{3,2,1,0:T(8,128)(2,1)S(1)} %collective-permute-done.1.earlier, bf16[2,8,2,96,128]{4,3,2,1,0:T(8,128)(2,1)S(1)} %bitcast.7, ...), custom_call_target="tpu_custom_call" | custom-call | flops 1048576 | bytes 1024 | tf_op jit(solution)/shard_map/pallas_call | solution.py:219
  27.0 2.7 %collective-permute-done.refs_0_ = bf16[4,2,96,128]{3,2,1,0:T(8,128)(2,1)S(1)} collective-permute-done((bf16[4,2,96,128]{3,2,1,0:T(8,128)(2,1)S(1)}, bf16[4,2,96,128]{3,2,1,0:T(8,128)(2,1)S(1)}, u32[]{:S(2)}, u32[]{:S(2)}) %collective-permute-start) | collective-permute-done | bytes 196640 | tf_op jit(solution)/shard_map/ppermute | solution.py:280
  29.7 1.3 %collective-permute-start.4 = (bf16[4,2,96,128]{3,2,1,0:T(8,128)(2,1)S(1)}, bf16[4,2,96,128]{3,2,1,0:T(8,128)(2,1)S(1)}, u32[]{:S(2)}, u32[]{:S(2)}) collective-permute-start(bf16[4,2,96,128]{3,2,1,0:T(8,128)(2,1)S(1)} %shard_map.76), channel_id=1, source_target_pairs={{0,64},{1,65},{2,66},{3,67},{4,68},{5,69},{6,70},{7,71},{8,72},{9,... | collective-permute-start | bytes 589832 | tf_op jit(solution)/shard_map/ppermute | solution.py:298
  31.0 0.0 collective-permute-done.3.refs_0_
  31.0 1.3 %collective-permute-start.5 = (bf16[4,2,96,128]{3,2,1,0:T(8,128)(2,1)S(1)}, bf16[4,2,96,128]{3,2,1,0:T(8,128)(2,1)S(1)}, u32[]{:S(2)}, u32[]{:S(2)}) collective-permute-start(bf16[4,2,96,128]{3,2,1,0:T(8,128)(2,1)S(1)} %shard_map.77.refs_2_), channel_id=1, source_target_pairs={{95,159},{96,160},{223,287},{224,288},{415,479},{416,480}} | collective-permute-start | bytes 589832 | tf_op jit(solution)/shard_map/ppermute | solution.py:298
  32.3 0.0 collective-permute-done.2.refs_0_
  32.3 0.7 %collective-permute-start.6 = (bf16[4,2,96,128]{3,2,1,0:T(8,128)(2,1)S(1)}, bf16[4,2,96,128]{3,2,1,0:T(8,128)(2,1)S(1)}, u32[]{:S(2)}, u32[]{:S(2)}) collective-permute-start(bf16[4,2,96,128]{3,2,1,0:T(8,128)(2,1)S(1)} %shard_map.78), channel_id=1, source_target_pairs={{287,351},{288,352}} | collective-permute-start | bytes 589832 | tf_op jit(solution)/shard_map/ppermute | solution.py:298
  33.0 1.4 %shard_map.80 = (bf16[2,2,96,128]{3,2,1,0:T(8,128)(2,1)S(1)}, f32[4,2,96,128]{3,2,1,0:T(8,128)S(1)}, f32[4,2,96,128]{3,2,1,0:T(8,128)S(1)}) custom-call(bf16[4,4,96,128]{3,2,1,0:T(8,128)(2,1)S(1)} %shard_map.74.own, bf16[4,4,96,128]{3,2,1,0:T(8,128)(2,1)S(1)} %collective-permute-done.1.earlier, bf16[4,2,96,128]{3,2,1,0:T(8,128)(2,1)S(1)} %add_add_fusion.far, ...), custom_call_target="tpu_custom_call" | custom-call | flops 1073741824 | bytes 2097152 | tf_op jit(solution)/shard_map/pallas_call | solution.py:219
  34.4 0.5 %collective-permute-done.4.refs_0_ = bf16[4,2,96,128]{3,2,1,0:T(8,128)(2,1)S(1)} collective-permute-done((bf16[4,2,96,128]{3,2,1,0:T(8,128)(2,1)S(1)}, bf16[4,2,96,128]{3,2,1,0:T(8,128)(2,1)S(1)}, u32[]{:S(2)}, u32[]{:S(2)}) %collective-permute-start.4) | collective-permute-done | bytes 196640 | tf_op jit(solution)/shard_map/ppermute | solution.py:298
  35.0 0.0 collective-permute-done.6.third_corner
  35.0 2.4 %collective-permute-done.5.second_corner = bf16[4,2,96,128]{3,2,1,0:T(8,128)(2,1)S(1)} collective-permute-done((bf16[4,2,96,128]{3,2,1,0:T(8,128)(2,1)S(1)}, bf16[4,2,96,128]{3,2,1,0:T(8,128)(2,1)S(1)}, u32[]{:S(2)}, u32[]{:S(2)}) %collective-permute-start.5) | collective-permute-done | bytes 196640 | tf_op jit(solution)/shard_map/ppermute | solution.py:298
  37.4 2.4 %shard_map.81 = bf16[1536,128]{1,0:T(8,128)(2,1)} custom-call(bf16[1536,128]{1,0:T(8,128)(2,1)S(1)} %get-tuple-element.18.features, bf16[4,2,96,128]{3,2,1,0:T(8,128)(2,1)S(1)} %add_add_fusion.far, bf16[4,2,96,128]{3,2,1,0:T(8,128)(2,1)S(1)} %shard_map.79.corner, bf16[4,2,96,128]{3,2,1,0:T(8,128)(2,1)S(1)} %collective-permute-done.5.second_corner, ...), custom_call_target="tpu_custom_call" | custom-call | flops 509607936 | bytes 2097152 | tf_op jit(solution)/shard_map/pallas_call | solution.py:219
  (8 shorter events, 0.1 us)
Async XLA Ops:
  0.0 19.9 %copy-start.1 = (bf16[96,2592]{1,0:T(8,128)(2,1)S(1)}, bf16[96,2592]{1,0:T(8,128)(2,1)}, u32[]{:S(2)}) copy-start(bf16[96,2592]{1,0:T(8,128)(2,1)} %first.1) | copy-start | bytes 1492996
  0.0 20.0 %copy-start.2 = (bf16[96,2592]{1,0:T(8,128)(2,1)S(1)}, bf16[96,2592]{1,0:T(8,128)(2,1)}, u32[]{:S(2)}) copy-start(bf16[96,2592]{1,0:T(8,128)(2,1)} %second.1) | copy-start | bytes 1492996
  1.6 18.3 %copy-start = (bf16[96,4,4,128]{3,2,1,0:T(4,128)(2,1)S(1)}, bf16[96,4,4,128]{3,2,1,0:T(4,128)(2,1)}, u32[]{:S(2)}) copy-start(bf16[96,4,4,128]{3,2,1,0:T(4,128)(2,1)} %param.7) | copy-start | bytes 1179652
  1.7 20.1 %collective-permute-start.1 = (bf16[4,4,96,128]{3,2,1,0:T(8,128)(2,1)S(1)}, bf16[4,4,96,128]{3,2,1,0:T(8,128)(2,1)S(1)}, u32[]{:S(2)}, u32[]{:S(2)}) collective-permute-start(bf16[4,4,96,128]{3,2,1,0:T(8,128)(2,1)S(1)} %shard_map.74.own), channel_id=1, source_target_pairs={{0,64},{64,128},{128,192},{192,256},{256,320},{320,384},{384,448},... | collective-permute-start | bytes 1179656 | tf_op jit(solution)/shard_map/ppermute | solution.py:288
  5.4 25.6 %collective-permute-start.3 = (bf16[4,2,96,128]{3,2,1,0:T(8,128)(2,1)S(1)}, bf16[4,2,96,128]{3,2,1,0:T(8,128)(2,1)S(1)}, u32[]{:S(2)}, u32[]{:S(2)}) collective-permute-start(bf16[4,2,96,128]{3,2,1,0:T(8,128)(2,1)S(1)} %get-tuple-element.32), channel_id=1, source_target_pairs={{95,96},{96,95},{223,224},{224,223},{415,416},{416,415}} | collective-permute-start | bytes 589832 | tf_op jit(solution)/shard_map/ppermute | solution.py:280
  6.1 26.2 %collective-permute-start.2 = (bf16[4,2,96,128]{3,2,1,0:T(8,128)(2,1)S(1)}, bf16[4,2,96,128]{3,2,1,0:T(8,128)(2,1)S(1)}, u32[]{:S(2)}, u32[]{:S(2)}) collective-permute-start(bf16[4,2,96,128]{3,2,1,0:T(8,128)(2,1)S(1)} %get-tuple-element.32), channel_id=1, source_target_pairs={{287,288},{288,287}} | collective-permute-start | bytes 589832 | tf_op jit(solution)/shard_map/ppermute | solution.py:280
  6.7 22.9 %collective-permute-start = (bf16[4,2,96,128]{3,2,1,0:T(8,128)(2,1)S(1)}, bf16[4,2,96,128]{3,2,1,0:T(8,128)(2,1)S(1)}, u32[]{:S(2)}, u32[]{:S(2)}) collective-permute-start(bf16[4,2,96,128]{3,2,1,0:T(8,128)(2,1)S(1)} %get-tuple-element.32), channel_id=1, source_target_pairs={{1,2},{3,4},{5,6},{7,8},{9,10},{11,12},{13,14},{15,16},{17,18},{19... | collective-permute-start | bytes 589832 | tf_op jit(solution)/shard_map/ppermute | solution.py:280
  19.9 0.7 %copy-start.3 = (f32[96]{0:T(128)S(1)}, f32[96]{0:T(128)}, u32[]{:S(2)}) copy-start(f32[96]{0:T(128)} %param.10) | copy-start | bytes 1156
  19.9 0.7 %copy-start.4 = (f32[96]{0:T(128)S(1)}, f32[96]{0:T(128)}, u32[]{:S(2)}) copy-start(f32[96]{0:T(128)} %param.11) | copy-start | bytes 1156
  19.9 0.7 %copy-start.5 = (f32[96]{0:T(128)S(1)}, f32[96]{0:T(128)}, u32[]{:S(2)}) copy-start(f32[96]{0:T(128)} %param.13) | copy-start | bytes 1156
  29.7 5.3 %collective-permute-start.4 = (bf16[4,2,96,128]{3,2,1,0:T(8,128)(2,1)S(1)}, bf16[4,2,96,128]{3,2,1,0:T(8,128)(2,1)S(1)}, u32[]{:S(2)}, u32[]{:S(2)}) collective-permute-start(bf16[4,2,96,128]{3,2,1,0:T(8,128)(2,1)S(1)} %shard_map.76), channel_id=1, source_target_pairs={{0,64},{1,65},{2,66},{3,67},{4,68},{5,69},{6,70},{7,71},{8,72},{9,... | collective-permute-start | bytes 589832 | tf_op jit(solution)/shard_map/ppermute | solution.py:298
  31.0 6.4 %collective-permute-start.5 = (bf16[4,2,96,128]{3,2,1,0:T(8,128)(2,1)S(1)}, bf16[4,2,96,128]{3,2,1,0:T(8,128)(2,1)S(1)}, u32[]{:S(2)}, u32[]{:S(2)}) collective-permute-start(bf16[4,2,96,128]{3,2,1,0:T(8,128)(2,1)S(1)} %shard_map.77.refs_2_), channel_id=1, source_target_pairs={{95,159},{96,160},{223,287},{224,288},{415,479},{416,480}} | collective-permute-start | bytes 589832 | tf_op jit(solution)/shard_map/ppermute | solution.py:298
  32.3 2.6 %collective-permute-start.6 = (bf16[4,2,96,128]{3,2,1,0:T(8,128)(2,1)S(1)}, bf16[4,2,96,128]{3,2,1,0:T(8,128)(2,1)S(1)}, u32[]{:S(2)}, u32[]{:S(2)}) collective-permute-start(bf16[4,2,96,128]{3,2,1,0:T(8,128)(2,1)S(1)} %shard_map.78), channel_id=1, source_target_pairs={{287,351},{288,352}} | collective-permute-start | bytes 589832 | tf_op jit(solution)/shard_map/ppermute | solution.py:298

commit v5 on v4

--- a/solution.py
+++ b/solution.py
@@ -25,7 +25,8 @@
 def activation(values, gain):
     mean_square = jnp.sum(values * values, axis=0, keepdims=True) * (1.0 / C)
     scaled = values * lax.rsqrt(mean_square + 1e-06) * gain
-    return scaled * (1.0 / (1.0 + jnp.exp(-scaled)))
+    half = 0.5 * scaled
+    return half + half * jnp.tanh(half)
 
 
 def natural(row):
@@ -100,7 +101,8 @@
     return lax.axis_index("tm") > 0, jnp.logical_not(outer)
 
 
-def near_kernel(own, earlier, even, first_weight, second_weight, columns, near_hidden, branch_out, hidden):
+def near_kernel(features, own, earlier, even, first_weight, second_weight, columns, near_hidden, base, hidden):
+    base[...] = features[...].astype(F32)
     started, _ = borders()
     bias, gain, last_bias = columns[0], columns[1], columns[2]
     partner = 1 - lax.rem(lax.axis_index("height"), 2)
@@ -130,7 +132,8 @@
             second_weight[...], window(inner, frame, range(1, 4)), window(inner, frame, range(2, 5))
         )
         for step, sums in enumerate(pair):
-            branch_out[frame, step] = sums + last_bias
+            lines = pl.ds(frame * 4 + natural(step + 2), C, stride=16)
+            base[lines, :] = base[lines, :] + (sums + last_bias)
 
 
 def partial_kernel(
@@ -168,7 +171,7 @@
 
 
 def far_kernel(
-    features, far, corner, second_corner, third_corner, far_hidden, near_branch, first_part, branch_part, first_weight, second_weight, columns,
+    base, far, corner, second_corner, third_corner, far_hidden, first_part, branch_part, first_weight, second_weight, columns,
     encoded, hidden, total,
 ):
     started, joined = borders()
@@ -196,9 +199,6 @@
                 if keep is not None:
                     result = jnp.where(keep, result, 0.0)
                 hidden[frame + later, step] = result.astype(BF16)
-    for frame in range(4):
-        for step in range(2):
-            total[pl.ds(frame * 4 + natural(step + 2), C, stride=16), :] = near_branch[frame, step]
     for frame in (0, 2):
         for step, rows in ((0, (-1, 0)), (1, (0,))):
             weight = second_weight[:, : len(rows) * 3 * C]
@@ -207,7 +207,9 @@
                 place = (frame + later) * 4 + natural(step)
                 total[pl.ds(place, C, stride=16), :] = sums + branch_part[frame + later, step]
 
-    encoded[...] = (features[...].astype(F32) + total[...]).astype(BF16)
+    low = lax.rem(lax.broadcasted_iota(jnp.int32, (C * 16, W), 0), 4) < 2
+    even_place = lax.rem(lax.axis_index("height"), 2) == 0
+    encoded[...] = (base[...] + jnp.where(low == even_place, total[...], 0.0)).astype(BF16)
 
 
 def shape(*dims, dtype=BF16):
@@ -288,9 +290,9 @@
     earlier = lax.ppermute(act, "tm", later)
     both = jnp.concatenate([earlier[:, 2:4], act[:, 2:4]], axis=0)
     even = lax.all_gather(both, "height", axis_index_groups=[[i, i + 1] for i in range(0, height, 2)])
-    near_hidden, near_branch = call(
-        near_kernel, [shape(6, 2, C, W), shape(4, 2, C, W, dtype=F32)], [pltpu.VMEM((6, 4, C, W), BF16)],
-        (act, earlier, even, first, second, columns),
+    near_hidden, base = call(
+        near_kernel, [shape(6, 2, C, W), shape(C * 16, W, dtype=F32)], [pltpu.VMEM((6, 4, C, W), BF16)],
+        (kept, act, earlier, even, first, second, columns),
         cost_estimate=pl.CostEstimate(flops=1 << 20, bytes_accessed=1 << 10, transcendentals=0),
     )
     fars[0], fars[1] = (held(far, 1 << 33, near_hidden) for far in fars[:2])
@@ -307,7 +309,7 @@
     encoded = call(
         far_kernel, shape(C * 16, W),
         [pltpu.VMEM((4, 2, C, W), BF16), pltpu.VMEM((C * 16, W), F32)],
-        (kept, far, *corners, far_hidden, near_branch, first_part, branch_part, first, second, columns),
+        (base, far, *corners, far_hidden, first_part, branch_part, first, second, columns),
         cost_estimate=pl.CostEstimate(flops=8 * W * C * TAPS * 6, bytes_accessed=1 << 21, transcendentals=0),
     )
     return encoded.reshape(features.shape)

time: 40.1 us -> 40 us (level)
  transfers between devices with their start and end apart: 7 -> 7, of which waited for: 3 -> 3; matrix products, arithmetic and copies ran while one was open for 0% -> 0% of each run, Pallas kernels for 13% -> 14%
where the time goes in v5:
time: 40 us; the launch traced here: 39.8 us
  starting transfers between devices  21.4 us (54%)
  Pallas kernels  9.51 us (24%)
  waiting for transfers between devices  5.49 us (14%)
  blocking collectives  2.37 us (6%)
  local copies, waits for them, and re-layouts  0.69 us (2%)
    ppermute x3, starting transfers between devices, local(): fars = [lax.ppermute(edge, ('tm', 'height'), pairs) for pairs in crossing]  14.5 us
    pallas_call x4, Pallas kernels, call(): pl.pallas_call(kernel, out_shape=out_shape, in_specs=[VMEM] * len(inputs)...  7.91 us
    ppermute x1, starting transfers between devices, local(): earlier = lax.ppermute(act, 'tm', later)  3.68 us
    ppermute x3, starting transfers between devices, local(): lax.ppermute(far, ('tm', 'height'), pairs)  3.26 us
    ppermute x3, waiting for transfers between devices, local(): lax.ppermute(far, ('tm', 'height'), pairs)  3 us
    ppermute x3, waiting for transfers between devices, local(): fars = [lax.ppermute(edge, ('tm', 'height'), pairs) for pairs in crossing]  2.49 us
    all_gather x1, blocking collectives, local(): lax.all_gather(both, 'height', axis_index_groups=[[i, i + 1] for i in ran...  2.37 us
    pallas_call x1, Pallas kernels, local(): pl.pallas_call(first_act_kernel, out_shape=shape(4, 4, C, W), in_specs=[p...  1.59 us
  transfers between devices with their start and end apart: 7, of which 3 were waited for; matrix products, arithmetic and copies ran while one was open for 0% of the time, Pallas kernels for 14%

profile of v5, /device:TPU:95, one launch (start us, length us, event | category | flops | bytes accessed | tf_op | source)
XLA Modules:
  0.0 39.8 jit_solution(17269616746440633121)
XLA Ops:
  0.0 0.0 copy-start.1
  0.0 0.0 copy-start.2
  0.0 1.6 %shard_map.74.own = bf16[4,4,96,128]{3,2,1,0:T(8,128)(2,1)S(1)} custom-call(bf16[1536,128]{1,0:T(8,128)(2,1)} %bitcast.8, f32[1,96]{1,0:T(1,128)} %bitcast.13), custom_call_target="tpu_custom_call" | custom-call | tf_op jit(solution)/shard_map/pallas_call | solution.py:269
  1.6 0.0 copy-start
  1.6 3.7 %collective-permute-start = (bf16[4,4,96,128]{3,2,1,0:T(8,128)(2,1)S(1)}, bf16[4,4,96,128]{3,2,1,0:T(8,128)(2,1)S(1)}, u32[]{:S(2)}, u32[]{:S(2)}) collective-permute-start(bf16[4,4,96,128]{3,2,1,0:T(8,128)(2,1)S(1)} %shard_map.74.own), channel_id=1, source_target_pairs={{0,64},{64,128},{128,192},{192,256},{256,320},{320,384},{384,448},... | collective-permute-start | bytes 1179656 | tf_op jit(solution)/shard_map/ppermute | solution.py:290
  5.3 0.7 %collective-permute-start.3 = (bf16[4,2,96,128]{3,2,1,0:T(8,128)(2,1)S(1)}, bf16[4,2,96,128]{3,2,1,0:T(8,128)(2,1)S(1)}, u32[]{:S(2)}, u32[]{:S(2)}) collective-permute-start(bf16[4,2,96,128]{3,2,1,0:T(8,128)(2,1)S(1)} %get-tuple-element.31), channel_id=1, source_target_pairs={{95,96},{96,95},{223,224},{224,223},{415,416},{416,415}} | collective-permute-start | bytes 589832 | tf_op jit(solution)/shard_map/ppermute | solution.py:282
  6.0 13.2 %collective-permute-start.1 = (bf16[4,2,96,128]{3,2,1,0:T(8,128)(2,1)S(1)}, bf16[4,2,96,128]{3,2,1,0:T(8,128)(2,1)S(1)}, u32[]{:S(2)}, u32[]{:S(2)}) collective-permute-start(bf16[4,2,96,128]{3,2,1,0:T(8,128)(2,1)S(1)} %get-tuple-element.31), channel_id=1, source_target_pairs={{1,2},{3,4},{5,6},{7,8},{9,10},{11,12},{13,14},{15,16},{17,18},{19... | collective-permute-start | bytes 589832 | tf_op jit(solution)/shard_map/ppermute | solution.py:282
  19.2 0.7 %collective-permute-start.2 = (bf16[4,2,96,128]{3,2,1,0:T(8,128)(2,1)S(1)}, bf16[4,2,96,128]{3,2,1,0:T(8,128)(2,1)S(1)}, u32[]{:S(2)}, u32[]{:S(2)}) collective-permute-start(bf16[4,2,96,128]{3,2,1,0:T(8,128)(2,1)S(1)} %get-tuple-element.31), channel_id=1, source_target_pairs={{287,288},{288,287}} | collective-permute-start | bytes 589832 | tf_op jit(solution)/shard_map/ppermute | solution.py:282
  19.9 0.0 copy-start.3
  19.9 0.0 copy-start.4
  19.9 0.0 copy-start.5
  19.9 0.0 copy-done.1
  19.9 0.0 copy-done.2
  19.9 0.0 copy-done
  19.9 0.6 %copy-done.3 = f32[96]{0:T(128)S(1)} copy-done((f32[96]{0:T(128)S(1)}, f32[96]{0:T(128)}, u32[]{:S(2)}) %copy-start.3) | copy-done | bytes 408
  20.5 0.0 copy-done.4
  20.5 0.0 copy-done.5
  20.6 1.1 %shard_map.73 = (bf16[288,864]{1,0:T(8,128)(2,1)S(1)}, bf16[288,576]{1,0:T(8,128)(2,1)S(1)}, bf16[288,288]{1,0:T(8,128)(2,1)S(1)}, bf16[288,864]{1,0:T(8,128)(2,...) custom-call(bf16[96,2592]{1,0:T(8,128)(2,1)S(1)} %copy-done.1, ...), custom_call_target="tpu_custom_call" | custom-call | flops 134217728 | bytes 2097152 | tf_op jit(solution)/shard_map/pallas_call | solution.py:221
  21.7 0.0 collective-permute-done.earlier
  21.8 2.4 %all-gather = bf16[16,2,96,128]{3,2,1,0:T(8,128)(2,1)S(1)} all-gather(bf16[8,2,96,128]{3,2,1,0:T(8,128)(2,1)S(1)} %pad_maximum_fusion), channel_id=2, replica_groups={{0,1},{2,3},{4,5},{6,7},{8,9},{10,11},{12,13},{14,15},{16,17},{18,19},{..., dimensions={0}, use_global_device_ids=true | all-gather | bytes 1179648 | tf_op jit(solution)/shard_map/all_gather | solution.py:292
  24.1 3.0 %shard_map.75 = (bf16[6,2,96,128]{3,2,1,0:T(8,128)(2,1)S(1)}, f32[1536,128]{1,0:T(8,128)S(1)}) custom-call(bf16[1536,128]{1,0:T(8,128)(2,1)S(1)} %get-tuple-element.18.features, bf16[4,4,96,128]{3,2,1,0:T(8,128)(2,1)S(1)} %shard_map.74.own, bf16[4,4,96,128]{3,2,1,0:T(8,128)(2,1)S(1)} %collective-permute-done.earlier, ...), custom_call_target="tpu_custom_call" | custom-call | flops 1048576 | bytes 1024 | tf_op jit(solution)/shard_map/pallas_call | solution.py:221
  27.2 2.5 %collective-permute-done.1.refs_0_ = bf16[4,2,96,128]{3,2,1,0:T(8,128)(2,1)S(1)} collective-permute-done((bf16[4,2,96,128]{3,2,1,0:T(8,128)(2,1)S(1)}, bf16[4,2,96,128]{3,2,1,0:T(8,128)(2,1)S(1)}, u32[]{:S(2)}, u32[]{:S(2)}) %collective-permute-start.1) | collective-permute-done | bytes 196640 | tf_op jit(solution)/shard_map/ppermute | solution.py:282
  29.6 1.3 %collective-permute-start.4 = (bf16[4,2,96,128]{3,2,1,0:T(8,128)(2,1)S(1)}, bf16[4,2,96,128]{3,2,1,0:T(8,128)(2,1)S(1)}, u32[]{:S(2)}, u32[]{:S(2)}) collective-permute-start(bf16[4,2,96,128]{3,2,1,0:T(8,128)(2,1)S(1)} %shard_map.76), channel_id=1, source_target_pairs={{0,64},{1,65},{2,66},{3,67},{4,68},{5,69},{6,70},{7,71},{8,72},{9,... | collective-permute-start | bytes 589832 | tf_op jit(solution)/shard_map/ppermute | solution.py:300
  30.9 0.0 collective-permute-done.3.refs_0_
  31.0 1.3 %collective-permute-start.5 = (bf16[4,2,96,128]{3,2,1,0:T(8,128)(2,1)S(1)}, bf16[4,2,96,128]{3,2,1,0:T(8,128)(2,1)S(1)}, u32[]{:S(2)}, u32[]{:S(2)}) collective-permute-start(bf16[4,2,96,128]{3,2,1,0:T(8,128)(2,1)S(1)} %shard_map.77.refs_2_), channel_id=1, source_target_pairs={{95,159},{96,160},{223,287},{224,288},{415,479},{416,480}} | collective-permute-start | bytes 589832 | tf_op jit(solution)/shard_map/ppermute | solution.py:300
  32.3 0.0 collective-permute-done.2.refs_0_
  32.3 0.7 %collective-permute-start.6 = (bf16[4,2,96,128]{3,2,1,0:T(8,128)(2,1)S(1)}, bf16[4,2,96,128]{3,2,1,0:T(8,128)(2,1)S(1)}, u32[]{:S(2)}, u32[]{:S(2)}) collective-permute-start(bf16[4,2,96,128]{3,2,1,0:T(8,128)(2,1)S(1)} %shard_map.78), channel_id=1, source_target_pairs={{287,351},{288,352}} | collective-permute-start | bytes 589832 | tf_op jit(solution)/shard_map/ppermute | solution.py:300
  33.0 1.4 %shard_map.80 = (bf16[2,2,96,128]{3,2,1,0:T(8,128)(2,1)S(1)}, f32[4,2,96,128]{3,2,1,0:T(8,128)S(1)}, f32[4,2,96,128]{3,2,1,0:T(8,128)S(1)}) custom-call(bf16[4,4,96,128]{3,2,1,0:T(8,128)(2,1)S(1)} %shard_map.74.own, bf16[4,4,96,128]{3,2,1,0:T(8,128)(2,1)S(1)} %collective-permute-done.earlier, bf16[4,2,96,128]{3,2,1,0:T(8,128)(2,1)S(1)} %add_add_fusion.far, ...), custom_call_target="tpu_custom_call" | custom-call | flops 1073741824 | bytes 2097152 | tf_op jit(solution)/shard_map/pallas_call | solution.py:221
  34.4 0.8 %collective-permute-done.4.refs_0_ = bf16[4,2,96,128]{3,2,1,0:T(8,128)(2,1)S(1)} collective-permute-done((bf16[4,2,96,128]{3,2,1,0:T(8,128)(2,1)S(1)}, bf16[4,2,96,128]{3,2,1,0:T(8,128)(2,1)S(1)}, u32[]{:S(2)}, u32[]{:S(2)}) %collective-permute-start.4) | collective-permute-done | bytes 196640 | tf_op jit(solution)/shard_map/ppermute | solution.py:300
  35.1 2.2 %collective-permute-done.5.second_corner = bf16[4,2,96,128]{3,2,1,0:T(8,128)(2,1)S(1)} collective-permute-done((bf16[4,2,96,128]{3,2,1,0:T(8,128)(2,1)S(1)}, bf16[4,2,96,128]{3,2,1,0:T(8,128)(2,1)S(1)}, u32[]{:S(2)}, u32[]{:S(2)}) %collective-permute-start.5) | collective-permute-done | bytes 196640 | tf_op jit(solution)/shard_map/ppermute | solution.py:300
  37.4 0.0 collective-permute-done.6.third_corner
  37.4 2.4 %shard_map.81 = bf16[1536,128]{1,0:T(8,128)(2,1)} custom-call(f32[1536,128]{1,0:T(8,128)S(1)} %get-tuple-element.22.base, bf16[4,2,96,128]{3,2,1,0:T(8,128)(2,1)S(1)} %add_add_fusion.far, bf16[4,2,96,128]{3,2,1,0:T(8,128)(2,1)S(1)} %shard_map.79.corner, bf16[4,2,96,128]{3,2,1,0:T(8,128)(2,1)S(1)} %collective-permute-done.5.second_corner, ...), custom_call_target="tpu_custom_call" | custom-call | flops 509607936 | bytes 2097152 | tf_op jit(solution)/shard_map/pallas_call | solution.py:221
  (8 shorter events, 0.1 us)
Async XLA Ops:
  0.0 19.9 %copy-start.1 = (bf16[96,2592]{1,0:T(8,128)(2,1)S(1)}, bf16[96,2592]{1,0:T(8,128)(2,1)}, u32[]{:S(2)}) copy-start(bf16[96,2592]{1,0:T(8,128)(2,1)} %first.1) | copy-start | bytes 1492996
  0.0 19.9 %copy-start.2 = (bf16[96,2592]{1,0:T(8,128)(2,1)S(1)}, bf16[96,2592]{1,0:T(8,128)(2,1)}, u32[]{:S(2)}) copy-start(bf16[96,2592]{1,0:T(8,128)(2,1)} %second.1) | copy-start | bytes 1492996
  1.6 18.3 %copy-start = (bf16[96,4,4,128]{3,2,1,0:T(4,128)(2,1)S(1)}, bf16[96,4,4,128]{3,2,1,0:T(4,128)(2,1)}, u32[]{:S(2)}) copy-start(bf16[96,4,4,128]{3,2,1,0:T(4,128)(2,1)} %param.7) | copy-start | bytes 1179652
  1.6 20.1 %collective-permute-start = (bf16[4,4,96,128]{3,2,1,0:T(8,128)(2,1)S(1)}, bf16[4,4,96,128]{3,2,1,0:T(8,128)(2,1)S(1)}, u32[]{:S(2)}, u32[]{:S(2)}) collective-permute-start(bf16[4,4,96,128]{3,2,1,0:T(8,128)(2,1)S(1)} %shard_map.74.own), channel_id=1, source_target_pairs={{0,64},{64,128},{128,192},{192,256},{256,320},{320,384},{384,448},... | collective-permute-start | bytes 1179656 | tf_op jit(solution)/shard_map/ppermute | solution.py:290
  5.3 25.6 %collective-permute-start.3 = (bf16[4,2,96,128]{3,2,1,0:T(8,128)(2,1)S(1)}, bf16[4,2,96,128]{3,2,1,0:T(8,128)(2,1)S(1)}, u32[]{:S(2)}, u32[]{:S(2)}) collective-permute-start(bf16[4,2,96,128]{3,2,1,0:T(8,128)(2,1)S(1)} %get-tuple-element.31), channel_id=1, source_target_pairs={{95,96},{96,95},{223,224},{224,223},{415,416},{416,415}} | collective-permute-start | bytes 589832 | tf_op jit(solution)/shard_map/ppermute | solution.py:282
  6.0 23.6 %collective-permute-start.1 = (bf16[4,2,96,128]{3,2,1,0:T(8,128)(2,1)S(1)}, bf16[4,2,96,128]{3,2,1,0:T(8,128)(2,1)S(1)}, u32[]{:S(2)}, u32[]{:S(2)}) collective-permute-start(bf16[4,2,96,128]{3,2,1,0:T(8,128)(2,1)S(1)} %get-tuple-element.31), channel_id=1, source_target_pairs={{1,2},{3,4},{5,6},{7,8},{9,10},{11,12},{13,14},{15,16},{17,18},{19... | collective-permute-start | bytes 589832 | tf_op jit(solution)/shard_map/ppermute | solution.py:282
  19.2 13.1 %collective-permute-start.2 = (bf16[4,2,96,128]{3,2,1,0:T(8,128)(2,1)S(1)}, bf16[4,2,96,128]{3,2,1,0:T(8,128)(2,1)S(1)}, u32[]{:S(2)}, u32[]{:S(2)}) collective-permute-start(bf16[4,2,96,128]{3,2,1,0:T(8,128)(2,1)S(1)} %get-tuple-element.31), channel_id=1, source_target_pairs={{287,288},{288,287}} | collective-permute-start | bytes 589832 | tf_op jit(solution)/shard_map/ppermute | solution.py:282
  19.9 0.7 %copy-start.3 = (f32[96]{0:T(128)S(1)}, f32[96]{0:T(128)}, u32[]{:S(2)}) copy-start(f32[96]{0:T(128)} %param.10) | copy-start | bytes 1156
  19.9 0.7 %copy-start.4 = (f32[96]{0:T(128)S(1)}, f32[96]{0:T(128)}, u32[]{:S(2)}) copy-start(f32[96]{0:T(128)} %param.11) | copy-start | bytes 1156
  19.9 0.7 %copy-start.5 = (f32[96]{0:T(128)S(1)}, f32[96]{0:T(128)}, u32[]{:S(2)}) copy-start(f32[96]{0:T(128)} %param.13) | copy-start | bytes 1156
  29.6 5.5 %collective-permute-start.4 = (bf16[4,2,96,128]{3,2,1,0:T(8,128)(2,1)S(1)}, bf16[4,2,96,128]{3,2,1,0:T(8,128)(2,1)S(1)}, u32[]{:S(2)}, u32[]{:S(2)}) collective-permute-start(bf16[4,2,96,128]{3,2,1,0:T(8,128)(2,1)S(1)} %shard_map.76), channel_id=1, source_target_pairs={{0,64},{1,65},{2,66},{3,67},{4,68},{5,69},{6,70},{7,71},{8,72},{9,... | collective-permute-start | bytes 589832 | tf_op jit(solution)/shard_map/ppermute | solution.py:300
  31.0 6.4 %collective-permute-start.5 = (bf16[4,2,96,128]{3,2,1,0:T(8,128)(2,1)S(1)}, bf16[4,2,96,128]{3,2,1,0:T(8,128)(2,1)S(1)}, u32[]{:S(2)}, u32[]{:S(2)}) collective-permute-start(bf16[4,2,96,128]{3,2,1,0:T(8,128)(2,1)S(1)} %shard_map.77.refs_2_), channel_id=1, source_target_pairs={{95,159},{96,160},{223,287},{224,288},{415,479},{416,480}} | collective-permute-start | bytes 589832 | tf_op jit(solution)/shard_map/ppermute | solution.py:300
  32.3 5.1 %collective-permute-start.6 = (bf16[4,2,96,128]{3,2,1,0:T(8,128)(2,1)S(1)}, bf16[4,2,96,128]{3,2,1,0:T(8,128)(2,1)S(1)}, u32[]{:S(2)}, u32[]{:S(2)}) collective-permute-start(bf16[4,2,96,128]{3,2,1,0:T(8,128)(2,1)S(1)} %shard_map.78), channel_id=1, source_target_pairs={{287,351},{288,352}} | collective-permute-start | bytes 589832 | tf_op jit(solution)/shard_map/ppermute | solution.py:300

commit v6 on v5

--- a/solution.py
+++ b/solution.py
@@ -10,7 +10,7 @@
 C = 96
 W = 128
 TAPS = 9 * C
-TURNS = {1: 1, 3: 1, 6: 1, 4: 2}
+TURNS = {1: 1, 3: 1, 4: 1, 6: 1}
 BF16 = jnp.bfloat16
 F32 = jnp.float32
 VMEM = pl.BlockSpec(memory_space=pltpu.VMEM)
@@ -171,7 +171,7 @@
 
 
 def far_kernel(
-    base, far, corner, second_corner, third_corner, far_hidden, first_part, branch_part, first_weight, second_weight, columns,
+    base, far, corner, second_corner, far_hidden, first_part, branch_part, first_weight, second_weight, columns,
     encoded, hidden, total,
 ):
     started, joined = borders()
@@ -179,7 +179,7 @@
 
     def act(frame, row):
         if frame < 4:
-            return corner[frame, -1 - row] + second_corner[frame, -1 - row] + third_corner[frame, -1 - row]
+            return corner[frame, -1 - row] + second_corner[frame, -1 - row]
         return far[frame - 4, -1 - row]
 
     def outer(frame, row):
@@ -248,7 +248,7 @@
 
 def routes(times, height):
     middle = (height // 2 - 1, height // 2)
-    crossing, corner = [[], [], []], [[], [], []]
+    crossing, corner = [[], []], [[], []]
     for time in range(times):
         for a, b in swap_pairs(1, height):
             turn = TURNS.get(time, 0) if a in middle and b in middle else 0
@@ -295,11 +295,10 @@
         (kept, act, earlier, even, first, second, columns),
         cost_estimate=pl.CostEstimate(flops=1 << 20, bytes_accessed=1 << 10, transcendentals=0),
     )
-    fars[0], fars[1] = (held(far, 1 << 33, near_hidden) for far in fars[:2])
-    fars[2] = held(fars[2], 1 << 33, near_hidden, fars[1])
+    fars = [held(far, 1 << 33, near_hidden) for far in fars]
     corners = [lax.ppermute(far, ("tm", "height"), pairs) for far, pairs in zip(fars, corner)]
     corners[0] = held(corners[0], 1 << 28)
-    far = fars[0] + fars[2] + fars[1]
+    far = fars[0] + fars[1]
     far_hidden, first_part, branch_part = call(
         partial_kernel,
         [shape(2, 2, C, W), shape(4, 2, C, W, dtype=F32), shape(4, 2, C, W, dtype=F32)], [],

time: 40 us -> 41 us (1.025)
  the two profiles are of different devices: /device:TPU:95 before, /device:TPU:384 now
where the time goes in v6:
time: 41 us; the launch traced here: 40.8 us
  starting transfers between devices  14.7 us (36%)
  waiting for transfers between devices  13.3 us (32%)
  Pallas kernels  9.47 us (23%)
  blocking collectives  2.37 us (6%)
  local copies, waits for them, and re-layouts  0.69 us (2%)
    ppermute x2, starting transfers between devices, local(): fars = [lax.ppermute(edge, ('tm', 'height'), pairs) for pairs in crossing]  9.02 us
    pallas_call x4, Pallas kernels, call(): pl.pallas_call(kernel, out_shape=out_shape, in_specs=[VMEM] * len(inputs)...  7.88 us
    ppermute x2, waiting for transfers between devices, local(): fars = [lax.ppermute(edge, ('tm', 'height'), pairs) for pairs in crossing]  7.77 us
    ppermute x2, waiting for transfers between devices, local(): lax.ppermute(far, ('tm', 'height'), pairs)  5.39 us
    ppermute x1, starting transfers between devices, local(): earlier = lax.ppermute(act, 'tm', later)  3.06 us
    ppermute x2, starting transfers between devices, local(): lax.ppermute(far, ('tm', 'height'), pairs)  2.58 us
    all_gather x1, blocking collectives, local(): lax.all_gather(both, 'height', axis_index_groups=[[i, i + 1] for i in ran...  2.37 us
    pallas_call x1, Pallas kernels, local(): pl.pallas_call(first_act_kernel, out_shape=shape(4, 4, C, W), in_specs=[p...  1.59 us
  transfers between devices with their start and end apart: 5, of which 3 were waited for; matrix products, arithmetic and copies ran while one was open for 0% of the time, Pallas kernels for 13%

profile of v6, /device:TPU:384, one launch (start us, length us, event | category | flops | bytes accessed | tf_op | source)
XLA Modules:
  0.0 40.8 jit_solution(4285875278453015179)
XLA Ops:
  0.0 0.0 copy-start.1
  0.0 0.0 copy-start.2
  0.0 1.6 %shard_map.74.own = bf16[4,4,96,128]{3,2,1,0:T(8,128)(2,1)S(1)} custom-call(bf16[1536,128]{1,0:T(8,128)(2,1)} %bitcast.8, f32[1,96]{1,0:T(1,128)} %bitcast.13), custom_call_target="tpu_custom_call" | custom-call | tf_op jit(solution)/shard_map/pallas_call | solution.py:269
  1.6 0.0 copy-start
  1.6 3.1 %collective-permute-start = (bf16[4,4,96,128]{3,2,1,0:T(8,128)(2,1)S(1)}, bf16[4,4,96,128]{3,2,1,0:T(8,128)(2,1)S(1)}, u32[]{:S(2)}, u32[]{:S(2)}) collective-permute-start(bf16[4,4,96,128]{3,2,1,0:T(8,128)(2,1)S(1)} %shard_map.74.own), channel_id=1, source_target_pairs={{0,64},{64,128},{128,192},{192,256},{256,320},{320,384},{384,448},... | collective-permute-start | bytes 1179656 | tf_op jit(solution)/shard_map/ppermute | solution.py:290
  4.7 0.7 %collective-permute-start.1 = (bf16[4,2,96,128]{3,2,1,0:T(8,128)(2,1)S(1)}, bf16[4,2,96,128]{3,2,1,0:T(8,128)(2,1)S(1)}, u32[]{:S(2)}, u32[]{:S(2)}) collective-permute-start(bf16[4,2,96,128]{3,2,1,0:T(8,128)(2,1)S(1)} %get-tuple-element.31), channel_id=1, source_target_pairs={{1,2},{3,4},{5,6},{7,8},{9,10},{11,12},{13,14},{15,16},{17,18},{19... | collective-permute-start | bytes 589832 | tf_op jit(solution)/shard_map/ppermute | solution.py:282
  5.4 8.3 %collective-permute-start.2 = (bf16[4,2,96,128]{3,2,1,0:T(8,128)(2,1)S(1)}, bf16[4,2,96,128]{3,2,1,0:T(8,128)(2,1)S(1)}, u32[]{:S(2)}, u32[]{:S(2)}) collective-permute-start(bf16[4,2,96,128]{3,2,1,0:T(8,128)(2,1)S(1)} %get-tuple-element.31), channel_id=1, source_target_pairs={{95,96},{96,95},{223,224},{224,223},{287,288},{288,287},{415,416},... | collective-permute-start | bytes 589832 | tf_op jit(solution)/shard_map/ppermute | solution.py:282
  13.7 0.0 copy-start.3
  13.8 0.0 copy-start.4
  13.8 0.0 copy-start.5
  13.8 0.0 copy-done.1
  13.8 0.0 copy-done.2
  13.8 0.0 copy-done
  13.8 0.6 %copy-done.3 = f32[96]{0:T(128)S(1)} copy-done((f32[96]{0:T(128)S(1)}, f32[96]{0:T(128)}, u32[]{:S(2)}) %copy-start.3) | copy-done | bytes 408
  14.4 0.0 copy-done.4
  14.4 0.0 copy-done.5
  14.4 1.1 %shard_map.73 = (bf16[288,864]{1,0:T(8,128)(2,1)S(1)}, bf16[288,576]{1,0:T(8,128)(2,1)S(1)}, bf16[288,288]{1,0:T(8,128)(2,1)S(1)}, bf16[288,864]{1,0:T(8,128)(2,...) custom-call(bf16[96,2592]{1,0:T(8,128)(2,1)S(1)} %copy-done.1, ...), custom_call_target="tpu_custom_call" | custom-call | flops 134217728 | bytes 2097152 | tf_op jit(solution)/shard_map/pallas_call | solution.py:221
  15.5 0.2 collective-permute-done.earlier
  15.8 2.4 %all-gather = bf16[16,2,96,128]{3,2,1,0:T(8,128)(2,1)S(1)} all-gather(bf16[8,2,96,128]{3,2,1,0:T(8,128)(2,1)S(1)} %pad_maximum_fusion), channel_id=2, replica_groups={{0,1},{2,3},{4,5},{6,7},{8,9},{10,11},{12,13},{14,15},{16,17},{18,19},{..., dimensions={0}, use_global_device_ids=true | all-gather | bytes 1179648 | tf_op jit(solution)/shard_map/all_gather | solution.py:292
  18.1 3.0 %shard_map.75 = (bf16[6,2,96,128]{3,2,1,0:T(8,128)(2,1)S(1)}, f32[1536,128]{1,0:T(8,128)S(1)}) custom-call(bf16[1536,128]{1,0:T(8,128)(2,1)S(1)} %get-tuple-element.18.features, bf16[4,4,96,128]{3,2,1,0:T(8,128)(2,1)S(1)} %shard_map.74.own, bf16[4,4,96,128]{3,2,1,0:T(8,128)(2,1)S(1)} %collective-permute-done.earlier, ...), custom_call_target="tpu_custom_call" | custom-call | flops 1048576 | bytes 1024 | tf_op jit(solution)/shard_map/pallas_call | solution.py:221
  21.2 0.0 collective-permute-done.1.refs_0_
  21.2 0.7 %collective-permute-start.3 = (bf16[4,2,96,128]{3,2,1,0:T(8,128)(2,1)S(1)}, bf16[4,2,96,128]{3,2,1,0:T(8,128)(2,1)S(1)}, u32[]{:S(2)}, u32[]{:S(2)}) collective-permute-start(bf16[4,2,96,128]{3,2,1,0:T(8,128)(2,1)S(1)} %shard_map.76), channel_id=1, source_target_pairs={{0,64},{1,65},{2,66},{3,67},{4,68},{5,69},{6,70},{7,71},{8,72},{9,... | collective-permute-start | bytes 589832 | tf_op jit(solution)/shard_map/ppermute | solution.py:299
  21.9 7.8 %collective-permute-done.2.refs_0_ = bf16[4,2,96,128]{3,2,1,0:T(8,128)(2,1)S(1)} collective-permute-done((bf16[4,2,96,128]{3,2,1,0:T(8,128)(2,1)S(1)}, bf16[4,2,96,128]{3,2,1,0:T(8,128)(2,1)S(1)}, u32[]{:S(2)}, u32[]{:S(2)}) %collective-permute-start.2) | collective-permute-done | bytes 196640 | tf_op jit(solution)/shard_map/ppermute | solution.py:282
  29.6 1.9 %collective-permute-start.4 = (bf16[4,2,96,128]{3,2,1,0:T(8,128)(2,1)S(1)}, bf16[4,2,96,128]{3,2,1,0:T(8,128)(2,1)S(1)}, u32[]{:S(2)}, u32[]{:S(2)}) collective-permute-start(bf16[4,2,96,128]{3,2,1,0:T(8,128)(2,1)S(1)} %shard_map.77), channel_id=1, source_target_pairs={{95,159},{96,160},{223,287},{224,288},{287,351},{288,352},{415,479... | collective-permute-start | bytes 589832 | tf_op jit(solution)/shard_map/ppermute | solution.py:299
  31.6 0.1 add.3.far
  31.6 1.4 %shard_map.79 = (bf16[2,2,96,128]{3,2,1,0:T(8,128)(2,1)S(1)}, f32[4,2,96,128]{3,2,1,0:T(8,128)S(1)}, f32[4,2,96,128]{3,2,1,0:T(8,128)S(1)}) custom-call(bf16[4,4,96,128]{3,2,1,0:T(8,128)(2,1)S(1)} %shard_map.74.own, bf16[4,4,96,128]{3,2,1,0:T(8,128)(2,1)S(1)} %collective-permute-done.earlier, bf16[4,2,96,128]{3,2,1,0:T(8,128)(2,1)S(1)} %add.3.far, ...), custom_call_target="tpu_custom_call" | custom-call | flops 1073741824 | bytes 2097152 | tf_op jit(solution)/shard_map/pallas_call | solution.py:221
  33.0 0.0 collective-permute-done.3.refs_0_
  33.0 5.4 %collective-permute-done.4.second_corner = bf16[4,2,96,128]{3,2,1,0:T(8,128)(2,1)S(1)} collective-permute-done((bf16[4,2,96,128]{3,2,1,0:T(8,128)(2,1)S(1)}, bf16[4,2,96,128]{3,2,1,0:T(8,128)(2,1)S(1)}, u32[]{:S(2)}, u32[]{:S(2)}) %collective-permute-start.4) | collective-permute-done | bytes 196640 | tf_op jit(solution)/shard_map/ppermute | solution.py:299
  38.4 2.4 %shard_map.80 = bf16[1536,128]{1,0:T(8,128)(2,1)} custom-call(f32[1536,128]{1,0:T(8,128)S(1)} %get-tuple-element.22.base, bf16[4,2,96,128]{3,2,1,0:T(8,128)(2,1)S(1)} %add.3.far, bf16[4,2,96,128]{3,2,1,0:T(8,128)(2,1)S(1)} %shard_map.78.corner, bf16[4,2,96,128]{3,2,1,0:T(8,128)(2,1)S(1)} %collective-permute-done.4.second_corner, ...), custom_call_target="tpu_custom_call" | custom-call | flops 509607936 | bytes 2097152 | tf_op jit(solution)/shard_map/pallas_call | solution.py:221
  (6 shorter events, 0.1 us)
Async XLA Ops:
  0.0 13.8 %copy-start.1 = (bf16[96,2592]{1,0:T(8,128)(2,1)S(1)}, bf16[96,2592]{1,0:T(8,128)(2,1)}, u32[]{:S(2)}) copy-start(bf16[96,2592]{1,0:T(8,128)(2,1)} %first.1) | copy-start | bytes 1492996
  0.0 13.8 %copy-start.2 = (bf16[96,2592]{1,0:T(8,128)(2,1)S(1)}, bf16[96,2592]{1,0:T(8,128)(2,1)}, u32[]{:S(2)}) copy-start(bf16[96,2592]{1,0:T(8,128)(2,1)} %second.1) | copy-start | bytes 1492996
  1.6 12.2 %copy-start = (bf16[96,4,4,128]{3,2,1,0:T(4,128)(2,1)S(1)}, bf16[96,4,4,128]{3,2,1,0:T(4,128)(2,1)}, u32[]{:S(2)}) copy-start(bf16[96,4,4,128]{3,2,1,0:T(4,128)(2,1)} %param.7) | copy-start | bytes 1179652
  1.6 14.1 %collective-permute-start = (bf16[4,4,96,128]{3,2,1,0:T(8,128)(2,1)S(1)}, bf16[4,4,96,128]{3,2,1,0:T(8,128)(2,1)S(1)}, u32[]{:S(2)}, u32[]{:S(2)}) collective-permute-start(bf16[4,4,96,128]{3,2,1,0:T(8,128)(2,1)S(1)} %shard_map.74.own), channel_id=1, source_target_pairs={{0,64},{64,128},{128,192},{192,256},{256,320},{320,384},{384,448},... | collective-permute-start | bytes 1179656 | tf_op jit(solution)/shard_map/ppermute | solution.py:290
  4.7 16.4 %collective-permute-start.1 = (bf16[4,2,96,128]{3,2,1,0:T(8,128)(2,1)S(1)}, bf16[4,2,96,128]{3,2,1,0:T(8,128)(2,1)S(1)}, u32[]{:S(2)}, u32[]{:S(2)}) collective-permute-start(bf16[4,2,96,128]{3,2,1,0:T(8,128)(2,1)S(1)} %get-tuple-element.31), channel_id=1, source_target_pairs={{1,2},{3,4},{5,6},{7,8},{9,10},{11,12},{13,14},{15,16},{17,18},{19... | collective-permute-start | bytes 589832 | tf_op jit(solution)/shard_map/ppermute | solution.py:282
  5.4 24.2 %collective-permute-start.2 = (bf16[4,2,96,128]{3,2,1,0:T(8,128)(2,1)S(1)}, bf16[4,2,96,128]{3,2,1,0:T(8,128)(2,1)S(1)}, u32[]{:S(2)}, u32[]{:S(2)}) collective-permute-start(bf16[4,2,96,128]{3,2,1,0:T(8,128)(2,1)S(1)} %get-tuple-element.31), channel_id=1, source_target_pairs={{95,96},{96,95},{223,224},{224,223},{287,288},{288,287},{415,416},... | collective-permute-start | bytes 589832 | tf_op jit(solution)/shard_map/ppermute | solution.py:282
  13.7 0.7 %copy-start.3 = (f32[96]{0:T(128)S(1)}, f32[96]{0:T(128)}, u32[]{:S(2)}) copy-start(f32[96]{0:T(128)} %param.10) | copy-start | bytes 1156
  13.8 0.7 %copy-start.4 = (f32[96]{0:T(128)S(1)}, f32[96]{0:T(128)}, u32[]{:S(2)}) copy-start(f32[96]{0:T(128)} %param.11) | copy-start | bytes 1156
  13.8 0.7 %copy-start.5 = (f32[96]{0:T(128)S(1)}, f32[96]{0:T(128)}, u32[]{:S(2)}) copy-start(f32[96]{0:T(128)} %param.13) | copy-start | bytes 1156
  21.2 11.8 %collective-permute-start.3 = (bf16[4,2,96,128]{3,2,1,0:T(8,128)(2,1)S(1)}, bf16[4,2,96,128]{3,2,1,0:T(8,128)(2,1)S(1)}, u32[]{:S(2)}, u32[]{:S(2)}) collective-permute-start(bf16[4,2,96,128]{3,2,1,0:T(8,128)(2,1)S(1)} %shard_map.76), channel_id=1, source_target_pairs={{0,64},{1,65},{2,66},{3,67},{4,68},{5,69},{6,70},{7,71},{8,72},{9,... | collective-permute-start | bytes 589832 | tf_op jit(solution)/shard_map/ppermute | solution.py:299
  29.6 8.8 %collective-permute-start.4 = (bf16[4,2,96,128]{3,2,1,0:T(8,128)(2,1)S(1)}, bf16[4,2,96,128]{3,2,1,0:T(8,128)(2,1)S(1)}, u32[]{:S(2)}, u32[]{:S(2)}) collective-permute-start(bf16[4,2,96,128]{3,2,1,0:T(8,128)(2,1)S(1)} %shard_map.77), channel_id=1, source_target_pairs={{95,159},{96,160},{223,287},{224,288},{287,351},{288,352},{415,479... | collective-permute-start | bytes 589832 | tf_op jit(solution)/shard_map/ppermute | solution.py:299
